TPU v7x, 256 devices: a whole 4x4x8 slice. The times are simulated.
256 devices in a mesh: dp: 8 (over x, core), expert: 32 (over y, z).
Axes of the slice: x: 4, y: 4, z: 8, core: 2. Of those that a mesh axis runs over, the one named last changes fastest.
Arguments:
- tokens: bfloat16 [49152, 1024], P(('dp', 'expert')), may hold values from -6 to 6
- route_ids: int32 [49152, 4], P(('dp', 'expert')), may hold values from 0 to 31, all different within a row; in each aligned block of 192 rows (0 to 191, 192 to 383, ...) at most 36 rows name the same one
- gate_weight: float32 [49152, 4], P(('dp', 'expert')), may hold values from 0.25 to 1
- old_owner: int32 [32], replicated, may hold values from 0 to 31, as said below
- new_owner: int32 [32], replicated, may hold values from 0 to 31, as said below
- weights: bfloat16 [32, 3, 1024, 1024], P('expert', None, None, 'dp'), may hold values from -0.1875 to 0.1875
- first_moment: float32 [32, 3, 1024, 1024], P('expert', None, None, 'dp'), may hold values from -6 to 6
- second_moment: float32 [32, 3, 1024, 1024], P('expert', None, None, 'dp'), may hold values from 0.01 to 4
Outputs:
- layer_output: bfloat16 [49152, 1024], P(('dp', 'expert'))
- new_weights: bfloat16 [32, 3, 1024, 1024], P('expert', None, None, 'dp')
- new_first_moment: float32 [32, 3, 1024, 1024], P('expert', None, None, 'dp')
- new_second_moment: float32 [32, 3, 1024, 1024], P('expert', None, None, 'dp')
Inputs may be any that keep to these rules, and one draw needn't show every extreme that they name: `old_owner`: A permutation of the slots. `new_owner`: A permutation of the slots that differs from old_owner in exactly 5 experts. `route_ids`: the 4 experts of a row differ. In the 192 rows of one device no expert is named more than 36 times, a bound that some block reaches.
All inputs are finite; a program needn't handle non-finite values.
Results may differ from a plain program's by a relative error of at most 0.0058.
Values may be sent and summed in bfloat16 or wider, within the bound.
A program may use at most 128 MiB of HBM per device.

v0:
```python
import jax
import jax.numpy as jnp
from jax import lax
from jax.sharding import PartitionSpec as P


def relocate_weights(weights, source_slot):
    spread = lax.all_to_all(weights, "expert", split_axis=2, concat_axis=0, tiled=True)
    ordered = jnp.take(spread, source_slot, axis=0)
    return lax.all_to_all(ordered, "expert", split_axis=0, concat_axis=2, tiled=True)


def relocate_moments(first_moment, second_moment, source_slot):
    spread = (
        lax.all_to_all(first_moment, "expert", split_axis=2, concat_axis=0, tiled=True),
        lax.all_to_all(second_moment, "expert", split_axis=2, concat_axis=0, tiled=True),
    )
    ordered = (jnp.take(spread[0], source_slot, axis=0), jnp.take(spread[1], source_slot, axis=0))
    back = (
        lax.all_to_all(ordered[0], "expert", split_axis=0, concat_axis=2, tiled=True),
        lax.all_to_all(ordered[1], "expert", split_axis=0, concat_axis=2, tiled=True),
    )
    return (back[0], back[1])


def per_device(
    tokens, route_ids, gate_weight, old_owner, new_owner, weights, first_moment, second_moment
):
    peer_count = lax.axis_size("expert")
    tok_rows = tokens.shape[0]
    top_count = route_ids.shape[1]
    experts = old_owner.shape[0]
    capacity = max(2, 3 * tok_rows * top_count // (2 * experts))
    labels = jnp.arange(experts, dtype=jnp.int32)
    source_slot = jnp.sum(
        jnp.where(new_owner[None, :] == labels[:, None], old_owner[None, :], 0), axis=1
    )
    moved_first, moved_second = relocate_moments(first_moment, second_moment, source_slot)
    moved_weights = relocate_weights(weights, source_slot)
    expert_ids = route_ids.reshape(-1)
    target = jnp.sum(
        jnp.where(expert_ids[:, None] == labels[None, :], new_owner[None, :], 0), axis=1
    )
    matches = (target[:, None] == labels[None, :]).astype(jnp.int32)
    position = jnp.sum((jnp.cumsum(matches, axis=0) - 1) * matches, axis=1)
    slot_index = target * capacity + position
    slot_grid = slot_index.reshape(tok_rows, top_count)
    buffer_slots = jnp.arange(peer_count * capacity, dtype=jnp.int32)
    placement = jnp.any(slot_grid[None, :, :] == buffer_slots[:, None, None], axis=2).astype(
        jnp.bfloat16
    )
    outgoing = jnp.dot(placement, tokens, preferred_element_type=jnp.float32).astype(jnp.bfloat16)
    outgoing = outgoing.reshape(peer_count, capacity, tokens.shape[1])
    incoming = lax.all_to_all(outgoing, "expert", split_axis=0, concat_axis=0, tiled=True)
    received_rows = incoming.reshape(peer_count * capacity, tokens.shape[1])
    shard_piece = lax.all_gather(moved_weights, "dp", axis=3, tiled=True)
    gate_part = jnp.dot(received_rows, shard_piece[0, 0], preferred_element_type=jnp.float32)
    up_part = jnp.dot(received_rows, shard_piece[0, 1], preferred_element_type=jnp.float32)
    hidden = (jax.nn.silu(gate_part) * up_part).astype(jnp.bfloat16)
    accumulated = jnp.einsum(
        "rh,dh->rd", hidden, shard_piece[0, 2], preferred_element_type=jnp.float32
    )
    answers = accumulated.astype(jnp.bfloat16).reshape(peer_count, capacity, tokens.shape[1])
    returned = lax.all_to_all(answers, "expert", split_axis=0, concat_axis=0, tiled=True)
    returned = returned.reshape(peer_count * capacity, tokens.shape[1])
    picked = (
        jnp.take(returned, slot_index, axis=0)
        .astype(jnp.float32)
        .reshape(tok_rows, top_count, tokens.shape[1])
    )
    layer_output = jnp.sum(picked * gate_weight[:, :, None], axis=1).astype(jnp.bfloat16)
    return (layer_output, moved_weights, moved_first, moved_second)


def solution(mesh):
    placed = (
        P(("dp", "expert"), None),
        P(("dp", "expert"), None),
        P(("dp", "expert"), None),
        P(),
        P(),
        P("expert", None, None, "dp"),
        P("expert", None, None, "dp"),
        P("expert", None, None, "dp"),
    )
    return jax.shard_map(
        per_device,
        mesh=mesh,
        in_specs=placed,
        out_specs=(
            P(("dp", "expert"), None),
            P("expert", None, None, "dp"),
            P("expert", None, None, "dp"),
            P("expert", None, None, "dp"),
        ),
        check_vma=False,
    )
```

profile of v0, /device:TPU:2, one launch (start us, length us, event | category | flops | bytes accessed | tf_op | source)
XLA Modules:
  0.0 434.6 jit_solution(15613152316707516499)
XLA Ops:
  10.0 11.5 %all-to-all-start.1 = ((bf16[1,3,1024,128]{3,1,0,2:T(4,128)(2,1)}), bf16[1,3,1024,128]{3,1,0,2:T(4,128)(2,1)S(1)}, u32[]{:S(2)}, u32[]{:S(2)}) async-start(bf16[1,3,1024,128]{3,1,0,2:T(4,128)(2,1)} %copy.43), calls=%async_computation.1 | async-start | bytes 2097152 | tf_op jit(solution)/shard_map/all_to_all | solution.py:8
  21.7 28.5 %all-to-all-done.1 = bf16[1,3,1024,128]{3,1,0,2:T(4,128)(2,1)S(1)} async-done(((bf16[1,3,1024,128]{3,1,0,2:T(4,128)(2,1)}), bf16[1,3,1024,128]{3,1,0,2:T(4,128)(2,1)S(1)}, u32[]{:S(2)}, u32[]{:S(2)}) %all-to-all-start.1) | async-done | bytes 786464 | tf_op jit(solution)/shard_map/all_to_all | solution.py:8
  52.0 5.1 %all-to-all-start.2 = ((bf16[32,3,32,128]{3,2,1,0:T(8,128)(2,1)}), bf16[32,3,32,128]{3,2,1,0:T(8,128)(2,1)S(1)}, u32[]{:S(2)}, u32[]{:S(2)}) async-start(bf16[32,3,32,128]{3,2,1,0:T(8,128)(2,1)} %broadcast_select_fusion.2), calls=%async_computation.2 | async-start | bytes 1572864 | tf_op jit(solution)/shard_map/all_to_all | solution.py:10
  57.1 3.8 copy.48
  61.0 19.0 %all-to-all-done.2 = bf16[32,3,32,128]{3,2,1,0:T(8,128)(2,1)S(1)} async-done(((bf16[32,3,32,128]{3,2,1,0:T(8,128)(2,1)}), bf16[32,3,32,128]{3,2,1,0:T(8,128)(2,1)S(1)}, u32[]{:S(2)}, u32[]{:S(2)}) %all-to-all-start.2) | async-done | bytes 786464 | tf_op jit(solution)/shard_map/all_to_all | solution.py:10
  79.9 4.8 %all-to-all-start.4 = ((f32[1,3,1024,128]{3,1,0,2:T(4,128)}), f32[1,3,1024,128]{3,1,0,2:T(4,128)S(1)}, u32[]{:S(2)}, u32[]{:S(2)}) async-start(f32[1,3,1024,128]{3,1,0,2:T(4,128)} %copy.48), calls=%async_computation.4 | async-start | bytes 4194304 | tf_op jit(solution)/shard_map/all_to_all | solution.py:15
  84.7 3.9 copy.52
  88.6 45.7 %all-to-all-done.4 = f32[1,3,1024,128]{3,1,0,2:T(4,128)S(1)} async-done(((f32[1,3,1024,128]{3,1,0,2:T(4,128)}), f32[1,3,1024,128]{3,1,0,2:T(4,128)S(1)}, u32[]{:S(2)}, u32[]{:S(2)}) %all-to-all-start.4) | async-done | bytes 1572896 | tf_op jit(solution)/shard_map/all_to_all | solution.py:15
  134.3 6.0 %all-to-all-start.6 = ((f32[1,3,1024,128]{3,1,0,2:T(4,128)}), f32[1,3,1024,128]{3,1,0,2:T(4,128)}, u32[]{:S(2)}, u32[]{:S(2)}) async-start(f32[1,3,1024,128]{3,1,0,2:T(4,128)} %copy.52), calls=%async_computation.6 | async-start | bytes 4194304 | tf_op jit(solution)/shard_map/all_to_all | solution.py:16
  147.7 42.2 %all-to-all-done.6 = f32[1,3,1024,128]{3,1,0,2:T(4,128)} async-done(((f32[1,3,1024,128]{3,1,0,2:T(4,128)}), f32[1,3,1024,128]{3,1,0,2:T(4,128)}, u32[]{:S(2)}, u32[]{:S(2)}) %all-to-all-start.6) | async-done | bytes 1572896 | tf_op jit(solution)/shard_map/all_to_all | solution.py:16
  189.9 6.0 %all-to-all-start = ((bf16[32,36,1024]{2,1,0:T(8,128)(2,1)}), bf16[32,36,1024]{2,1,0:T(8,128)(2,1)S(1)}, u32[]{:S(2)}, u32[]{:S(2)}) async-start(bf16[32,36,1024]{2,1,0:T(8,128)(2,1)} %reshape.119), calls=%async_computation | async-start | bytes 5242880 | tf_op jit(solution)/shard_map/all_to_all | solution.py:54
  201.8 3.2 gather_fusion.2
  208.2 4.1 broadcast_select_fusion
  212.4 46.4 %all-to-all-done = bf16[32,36,1024]{2,1,0:T(8,128)(2,1)S(1)} async-done(((bf16[32,36,1024]{2,1,0:T(8,128)(2,1)}), bf16[32,36,1024]{2,1,0:T(8,128)(2,1)S(1)}, u32[]{:S(2)}, u32[]{:S(2)}) %all-to-all-start) | async-done | bytes 2359328 | tf_op jit(solution)/shard_map/all_to_all | solution.py:54
  258.8 43.9 %all_to_all.118 = f32[32,3,32,128]{3,2,1,0:T(8,128)} all-to-all(f32[32,3,32,128]{3,2,1,0:T(8,128)} %get-tuple-element.6), channel_id=1, replica_groups=mesh['dp'=8,'expert'=32] {'expert'}, dimensions={0} | all-to-all | bytes 3145728 | tf_op jit(solution)/shard_map/all_to_all | solution.py:20
  302.7 5.2 %all-to-all-start.7 = ((f32[32,3,32,128]{3,2,1,0:T(8,128)}), f32[32,3,32,128]{3,2,1,0:T(8,128)}, u32[]{:S(2)}, u32[]{:S(2)}) async-start(f32[32,3,32,128]{3,2,1,0:T(8,128)} %get-tuple-element.5), calls=%async_computation.7 | async-start | bytes 3145728 | tf_op jit(solution)/shard_map/all_to_all | solution.py:21
  310.0 7.3 %fusion.2 = f32[1152,1024]{1,0:T(8,128)} fusion(bf16[1152,1024]{1,0:T(8,128)(2,1)} %reshape.120, bf16[1,3,1024,1024]{3,2,1,0:T(8,128)(2,1)} %all-gather.2.cloned.1.call-done), kind=kOutput, calls=%fused_computation.14 | convolution fusion | flops 2415919104 | bytes 9175040 | tf_op jit(solution)/shard_map/dot_general | solution.py:57
  317.3 10.2 %convolution_convert_fusion = bf16[1152,1024]{1,0:T(8,128)(2,1)} fusion(bf16[1,3,1024,1024]{3,2,1,0:T(8,128)(2,1)} %all-gather.2.cloned.1.call-done, bf16[1152,1024]{1,0:T(8,128)(2,1)S(1)} %copy-done.4, f32[1152,1024]{1,0:T(8,128)} %fusion.2), kind=kOutput, calls=%fused_computation.5 | convolution fusion | flops 4840095744 | bytes 13631488 | tf_op jit(solution)/shard_map/rh,dh->rd/dot_general | solution.py:60
  327.5 4.1 reshape.121
  331.6 15.0 %all-to-all-done.7 = f32[32,3,32,128]{3,2,1,0:T(8,128)} async-done(((f32[32,3,32,128]{3,2,1,0:T(8,128)}), f32[32,3,32,128]{3,2,1,0:T(8,128)}, u32[]{:S(2)}, u32[]{:S(2)}) %all-to-all-start.7) | async-done | bytes 1572896 | tf_op jit(solution)/shard_map/all_to_all | solution.py:21
  346.6 5.6 %all-to-all-start.3 = ((bf16[32,36,1024]{2,1,0:T(8,128)(2,1)}), bf16[32,36,1024]{2,1,0:T(8,128)(2,1)}, u32[]{:S(2)}, u32[]{:S(2)}) async-start(bf16[32,36,1024]{2,1,0:T(8,128)(2,1)} %reshape.121), calls=%async_computation.3 | async-start | bytes 5242880 | tf_op jit(solution)/shard_map/all_to_all | solution.py:64
  356.4 58.7 %all-to-all-done.3 = bf16[32,36,1024]{2,1,0:T(8,128)(2,1)} async-done(((bf16[32,36,1024]{2,1,0:T(8,128)(2,1)}), bf16[32,36,1024]{2,1,0:T(8,128)(2,1)}, u32[]{:S(2)}, u32[]{:S(2)}) %all-to-all-start.3) | async-done | bytes 2359328 | tf_op jit(solution)/shard_map/all_to_all | solution.py:64
  417.7 3.6 gather_fusion.1
  423.8 3.9 multiply_reduce_fusion
  (58 shorter events, 32.8 us)
Async XLA Ops:
  7.2 137.5 %copy-start = (bf16[192,1024]{1,0:T(8,128)(2,1)S(1)}, bf16[192,1024]{1,0:T(8,128)(2,1)}, u32[]{:S(2)}) copy-start(bf16[192,1024]{1,0:T(8,128)(2,1)} %param.10) | copy-start | bytes 1179652
  7.2 14.3 %copy-start.7 = (s32[32]{0:T(128)S(1)}, s32[32]{0:T(128)}, u32[]{:S(2)}) copy-start(s32[32]{0:T(128)} %param.14) | copy-start | bytes 388
  7.2 14.3 %copy-start.8 = (s32[32]{0:T(128)S(1)}, s32[32]{0:T(128)}, u32[]{:S(2)}) copy-start(s32[32]{0:T(128)} %param.13) | copy-start | bytes 388
  10.0 40.1 %all-to-all-start.1 = ((bf16[1,3,1024,128]{3,1,0,2:T(4,128)(2,1)}), bf16[1,3,1024,128]{3,1,0,2:T(4,128)(2,1)S(1)}, u32[]{:S(2)}, u32[]{:S(2)}) async-start(bf16[1,3,1024,128]{3,1,0,2:T(4,128)(2,1)} %copy.43), calls=%async_computation.1 | async-start | bytes 2097152 | tf_op jit(solution)/shard_map/all_to_all | solution.py:8
  52.0 27.9 %all-to-all-start.2 = ((bf16[32,3,32,128]{3,2,1,0:T(8,128)(2,1)}), bf16[32,3,32,128]{3,2,1,0:T(8,128)(2,1)S(1)}, u32[]{:S(2)}, u32[]{:S(2)}) async-start(bf16[32,3,32,128]{3,2,1,0:T(8,128)(2,1)} %broadcast_select_fusion.2), calls=%async_computation.2 | async-start | bytes 1572864 | tf_op jit(solution)/shard_map/all_to_all | solution.py:10
  79.9 54.3 %all-to-all-start.4 = ((f32[1,3,1024,128]{3,1,0,2:T(4,128)}), f32[1,3,1024,128]{3,1,0,2:T(4,128)S(1)}, u32[]{:S(2)}, u32[]{:S(2)}) async-start(f32[1,3,1024,128]{3,1,0,2:T(4,128)} %copy.48), calls=%async_computation.4 | async-start | bytes 4194304 | tf_op jit(solution)/shard_map/all_to_all | solution.py:15
  88.6 52.7 %copy-start.5 = (s32[192,4]{0,1:T(4,128)S(1)}, s32[192,4]{0,1:T(4,128)}, u32[]{:S(2)}) copy-start(s32[192,4]{0,1:T(4,128)} %param.11) | copy-start | bytes 9220
  134.3 7.0 %copy-start.2 = (f32[1,3,1024,128]{3,1,0,2:T(4,128)}, f32[1,3,1024,128]{3,1,0,2:T(4,128)S(1)}, u32[]{:S(2)}) copy-start(f32[1,3,1024,128]{3,1,0,2:T(4,128)S(1)} %all-to-all-done.4) | copy-start | bytes 4718596
  134.3 55.6 %all-to-all-start.6 = ((f32[1,3,1024,128]{3,1,0,2:T(4,128)}), f32[1,3,1024,128]{3,1,0,2:T(4,128)}, u32[]{:S(2)}, u32[]{:S(2)}) async-start(f32[1,3,1024,128]{3,1,0,2:T(4,128)} %copy.52), calls=%async_computation.6 | async-start | bytes 4194304 | tf_op jit(solution)/shard_map/all_to_all | solution.py:16
  140.2 169.8 %all-gather.2.cloned.1.call-start = ((), (), s32[]{:S(2)}) async-start(), calls=%async_computation.8 | async-start | bytes 7077888 | tf_op jit(solution)/shard_map/all_gather | solution.py:56
  189.9 68.9 %all-to-all-start = ((bf16[32,36,1024]{2,1,0:T(8,128)(2,1)}), bf16[32,36,1024]{2,1,0:T(8,128)(2,1)S(1)}, u32[]{:S(2)}, u32[]{:S(2)}) async-start(bf16[32,36,1024]{2,1,0:T(8,128)(2,1)} %reshape.119), calls=%async_computation | async-start | bytes 5242880 | tf_op jit(solution)/shard_map/all_to_all | solution.py:54
  302.7 43.9 %all-to-all-start.7 = ((f32[32,3,32,128]{3,2,1,0:T(8,128)}), f32[32,3,32,128]{3,2,1,0:T(8,128)}, u32[]{:S(2)}, u32[]{:S(2)}) async-start(f32[32,3,32,128]{3,2,1,0:T(8,128)} %get-tuple-element.5), calls=%async_computation.7 | async-start | bytes 3145728 | tf_op jit(solution)/shard_map/all_to_all | solution.py:21
  310.0 7.3 %copy-start.4 = (bf16[1152,1024]{1,0:T(8,128)(2,1)S(1)}, bf16[1152,1024]{1,0:T(8,128)(2,1)}, u32[]{:S(2)}) copy-start(bf16[1152,1024]{1,0:T(8,128)(2,1)} %reshape.120) | copy-start | bytes 7077892
  331.6 20.6 %copy-start.6 = (f32[192,4]{0,1:T(4,128)S(1)}, f32[192,4]{0,1:T(4,128)}, u32[]{:S(2)}) copy-start(f32[192,4]{0,1:T(4,128)} %param.12) | copy-start | bytes 9220
  331.6 20.8 %copy-start.3 = (f32[32,3,32,128]{3,2,1,0:T(8,128)S(1)}, f32[32,3,32,128]{3,2,1,0:T(8,128)}, u32[]{:S(2)}) copy-start(f32[32,3,32,128]{3,2,1,0:T(8,128)} %all_to_all.118) | copy-start | bytes 4718596
  346.6 68.5 %all-to-all-start.3 = ((bf16[32,36,1024]{2,1,0:T(8,128)(2,1)}), bf16[32,36,1024]{2,1,0:T(8,128)(2,1)}, u32[]{:S(2)}, u32[]{:S(2)}) async-start(bf16[32,36,1024]{2,1,0:T(8,128)(2,1)} %reshape.121), calls=%async_computation.3 | async-start | bytes 5242880 | tf_op jit(solution)/shard_map/all_to_all | solution.py:64
  417.7 10.0 %copy-start.1 = (bf16[192,1024]{1,0:T(8,128)(2,1)S(1)}, bf16[192,1024]{1,0:T(8,128)(2,1)}, u32[]{:S(2)}) copy-start(bf16[192,1024]{1,0:T(8,128)(2,1)} %param.10) | copy-start | bytes 1179652
Sparse Core Ops, SparseCore 0:
  143.5 48.5 all-gather.1
where the time goes:
time: 436 us; the launch traced here: 435 us
  waiting for transfers between devices  255 us (58%)
  local copies, waits for them, and re-layouts  46.6 us (11%)
  starting transfers between devices  44.1 us (10%)
  blocking collectives  43.9 us (10%)
  matrix products  18.3 us (4%)
  between operations  14.3 us (3%)
  other arithmetic  11.9 us (3%)
    all_to_all x1, waiting for transfers between devices, per_device(): lax.all_to_all(answers, 'expert', split_axis=0, concat_axis=0, tiled=True)  58.7 us
    all_to_all x1, waiting for transfers between devices, per_device(): lax.all_to_all(outgoing, 'expert', split_axis=0, concat_axis=0, tiled=True)  46.4 us
    all_to_all x1, waiting for transfers between devices, relocate_moments(): lax.all_to_all(first_moment, 'expert', split_axis=2, concat_axis=0, tiled...  45.7 us
    all_to_all x1, blocking collectives, relocate_moments(): lax.all_to_all(ordered[0], 'expert', split_axis=0, concat_axis=2, tiled=T...  43.9 us
    all_to_all x1, waiting for transfers between devices, relocate_moments(): lax.all_to_all(second_moment, 'expert', split_axis=2, concat_axis=0, tile...  42.2 us
    all_to_all x1, waiting for transfers between devices, relocate_weights(): lax.all_to_all(weights, 'expert', split_axis=2, concat_axis=0, tiled=True)  28.5 us
    all_to_all x1, waiting for transfers between devices, relocate_weights(): lax.all_to_all(ordered, 'expert', split_axis=0, concat_axis=2, tiled=True)  19 us
    all_to_all x1, waiting for transfers between devices, relocate_moments(): lax.all_to_all(ordered[1], 'expert', split_axis=0, concat_axis=2, tiled=T...  15 us
  transfers between devices with their start and end apart: 8, of which 7 were waited for; matrix products, arithmetic and copies ran while one was open for 14% of the time, Pallas kernels for 0%

commit v1 on v0

v1 whole, which is shorter than its diff:
```python
import functools

import jax
import jax.numpy as jnp
from jax import lax
from jax.experimental import pallas as pl
from jax.experimental.pallas import tpu as pltpu
from jax.sharding import PartitionSpec as P

MESH = pl.DeviceIdType.MESH
F32 = jnp.float32
BF16 = jnp.bfloat16
META = 16


class Plan:
    def __init__(self, n_dp, n_y, n_z, tok, cap, d, hs):
        self.nx, self.ny, self.nz = n_dp // 2, n_y, n_z
        self.tok, self.cap, self.d, self.hs = tok, cap, d, hs
        self.half = n_z // 2
        order = [0]
        for s in range(1, self.half):
            order += [s, n_z - s]
        order += [self.half]
        self.groups = (order[: self.half], order[self.half :])
        self.rows = self.half * cap
        self.yorder = [0, 1, 3, 2] if n_y == 4 else list(range(n_y))
        cut = tok // 2
        self.agcut = ((0, cut), (cut, tok + META - cut))
        self.rscut = ((0, cut), (cut, tok - cut))
        self.ag = [
            (way, part, s)
            for s in range(1, self.half + 1)
            for way in (0, 1)
            for part in (0, 1)
            if s < self.half or way == part
        ]
        self.rs = [
            (way, part, dist)
            for dist in range(self.half, 0, -1)
            for way in (0, 1)
            for part in (0, 1)
            if dist < self.half or way == part
        ]


def moe_kernel(
    p,
    tokx,
    wts,
    out,
    tokb,
    sendb,
    recvd,
    wall,
    res,
    rret,
    part,
    rsin,
    rsout,
    acc,
    prow,
    pcol,
    lsem,
    ags,
    agr,
    xs,
    xr,
    ds,
    dr,
    es,
    er,
    rss,
    rsr,
):
    ny, nz, nx = p.ny, p.nz, p.nx
    dp = lax.axis_index("dp")
    ex = lax.axis_index("expert")
    x, core = dp // 2, dp % 2
    y, z = ex // nz, ex % nz
    right = (dp, y * nz + (z + 1) % nz)
    left = (dp, y * nz + (z + nz - 1) % nz)
    above = [None] + [(dp, ((y + j) % ny) * nz + z) for j in range(1, ny)]
    twin = (x * 2 + 1 - core, ex)
    xright = (((x + 1) % nx) * 2 + core, ex)
    xleft = (((x + nx - 1) % nx) * 2 + core, ex)

    barrier = pltpu.get_barrier_semaphore()
    peers = [right, left, twin] + above[1:] + ([xright, xleft] if nx > 1 else [])
    for peer in peers:
        pl.semaphore_signal(barrier, inc=1, device_id=peer, device_id_type=MESH)
    pl.semaphore_wait(barrier, len(peers))

    def remote(src, dst, send, recv, to):
        return pltpu.make_async_remote_copy(
            src_ref=src, dst_ref=dst, send_sem=send, recv_sem=recv, device_id=to, device_id_type=MESH
        )

    started = []

    def go(copy):
        copy.start()
        started.append(copy)
        return copy

    def tok(r):
        return tokx if r == 0 else tokb.at[r - 1]

    def ag_copy(way, half, s):
        src = (nz - (s - 1)) % nz if way == 0 else s - 1
        dst = nz - s if way == 0 else s
        first, size = p.agcut[half]
        n = p.ag.index((way, half, s))
        return remote(
            tok(src).at[pl.ds(first, size)],
            tok(dst).at[pl.ds(first, size)],
            ags.at[n],
            agr.at[n],
            right if way == 0 else left,
        )

    agc = {}

    def ag_start(s):
        for way, half, step in p.ag:
            if step == s:
                if s > 1:
                    agc[way, half, s - 1].wait_recv()
                agc[way, half, s] = go(ag_copy(way, half, s))
        if s == p.half:
            for way in (0, 1):
                if s > 1:
                    agc[way, 1 - way, s - 1].wait_recv()

    ag_start(1)

    hd = p.d // 2
    keep = pltpu.make_async_copy(wts, wall.at[0, 0], lsem.at[0])
    keep.start()
    xc = [go(remote(wts, wall.at[0, 1], xs.at[0], xr.at[0], twin))]
    if nx > 1:
        xc.append(go(remote(wts, wall.at[3, 0], xs.at[1], xr.at[1], xright)))
        xc.append(go(remote(wts, wall.at[1, 0], xs.at[2], xr.at[2], xleft)))

    def x_second():
        if nx > 1:
            lo, hi = pl.ds(0, hd), pl.ds(hd, hd)
            xc[1].wait_recv()
            xc.append(go(remote(wall.at[3, 0, :, lo], wall.at[2, 0, :, lo], xs.at[3], xr.at[3], xright)))
            xc.append(go(remote(wall.at[3, 0], wall.at[3, 1], xs.at[4], xr.at[4], twin)))
            xc[2].wait_recv()
            xc.append(go(remote(wall.at[1, 0, :, hi], wall.at[2, 0, :, hi], xs.at[5], xr.at[5], xleft)))
            xc.append(go(remote(wall.at[1, 0], wall.at[1, 1], xs.at[6], xr.at[6], twin)))

    def x_third():
        if nx > 1:
            xc[3].wait_recv()
            xc[5].wait_recv()
            xc.append(go(remote(wall.at[2, 0], wall.at[2, 1], xs.at[7], xr.at[7], twin)))

    def x_ready():
        keep.wait()
        xc[0].wait_recv()
        if nx > 1:
            for n in (4, 6, 7):
                xc[n].wait_recv()

    tok_n = p.tok
    ta = lax.broadcasted_iota(jnp.int32, (tok_n, tok_n), 0)
    tb = lax.broadcasted_iota(jnp.int32, (tok_n, tok_n), 1)
    before = (ta < tb).astype(F32).astype(BF16)
    after = (tb < ta).astype(F32).astype(BF16)
    same = (ta == tb).astype(F32).astype(BF16)
    jrow = lax.broadcasted_iota(jnp.int32, (8, 1), 0)
    yrow = jnp.where(jrow + y >= ny, jrow + y - ny, jrow + y)
    column = jnp.where(jrow < ny, yrow * nz + z, -5).astype(F32)
    nt = (((1,), (1,)), ((), ()))

    def places(r):
        m = tok(r)[pl.ds(tok_n, META), pl.ds(0, tok_n)].astype(F32)
        named = jnp.zeros((8, tok_n), F32)
        ghi = jnp.zeros((8, tok_n), F32)
        glo = jnp.zeros((8, tok_n), F32)
        for k in range(4):
            hit = m[k : k + 1] == column
            named = named + jnp.where(hit, 1.0, 0.0)
            ghi = ghi + jnp.where(hit, m[4 + k : 5 + k], 0.0)
            glo = glo + jnp.where(hit, m[8 + k : 9 + k], 0.0)
        nb = named.astype(BF16)
        rank = jnp.dot(nb, before, preferred_element_type=F32)
        prow[r] = jnp.where(named > 0.5, rank, -4096.0)
        rank_c = lax.dot_general(after, nb, nt, preferred_element_type=F32)
        named_c = lax.dot_general(same, nb, nt, preferred_element_type=F32)
        gate_c = lax.dot_general(same, ghi.astype(BF16), nt, preferred_element_type=F32) + lax.dot_general(
            same, glo.astype(BF16), nt, preferred_element_type=F32
        )
        pcol[r, :, pl.ds(0, 8)] = jnp.where(named_c > 0.5, rank_c, -4096.0)
        pcol[r, :, pl.ds(8, 8)] = gate_c

    crow = lax.broadcasted_iota(jnp.int32, (p.rows, tok_n), 0).astype(F32)
    dc = {}
    nslot = 2 * ny

    def dispatch(h):
        for j in list(range(1, ny)) + [0]:
            total = jnp.zeros((p.rows, p.d), F32)
            for i, r in enumerate(p.groups[h]):
                pick = jnp.where(prow[r, j : j + 1, :] + float(i * p.cap) == crow, 1.0, 0.0).astype(BF16)
                total = total + jnp.dot(pick, tok(r)[pl.ds(0, tok_n)], preferred_element_type=F32)
            total = total.astype(BF16)
            if j == 0:
                recvd[pl.ds(h * ny * p.rows, p.rows)] = total
            else:
                n = h * (ny - 1) + j - 1
                sendb[n] = total
                pos = p.yorder.index((ny - j) % ny)
                dc[h, pos] = go(
                    remote(
                        sendb.at[n], recvd.at[pl.ds((h * ny + pos) * p.rows, p.rows)], ds.at[n], dr.at[n], above[j]
                    )
                )

    ec = {}

    def expert(h, first, count):
        base = (h * ny + first) * p.rows
        size = count * p.rows
        for pos in range(first, first + count):
            if pos > 0:
                dc[h, pos].wait_recv()

        def chunk(c, carry):
            xin = recvd[pl.ds(base, size)]
            wg = jnp.concatenate([wall[c, 0, 0], wall[c, 1, 0]], axis=1)
            wu = jnp.concatenate([wall[c, 0, 1], wall[c, 1, 1]], axis=1)
            wd = jnp.concatenate([wall[c, 0, 2], wall[c, 1, 2]], axis=1)
            g = jnp.dot(xin, wg, preferred_element_type=F32)
            u = jnp.dot(xin, wu, preferred_element_type=F32)
            hid = (g / (1.0 + jnp.exp(-g)) * u).astype(BF16)
            add = lax.dot_general(hid, wd, nt, preferred_element_type=F32)
            acc[pl.ds(0, size)] = acc[pl.ds(0, size)] + add
            return carry

        acc[pl.ds(0, size)] = jnp.zeros((size, p.d), F32)
        lax.fori_loop(0, nx, chunk, 0)
        res[pl.ds(base, size)] = acc[pl.ds(0, size)].astype(BF16)
        for pos in range(first, first + count):
            if pos > 0:
                o = p.yorder[pos]
                j = ny - o
                n = h * (ny - 1) + j - 1
                ec[h, j] = go(
                    remote(
                        res.at[pl.ds((h * ny + pos) * p.rows, p.rows)], rret.at[n], es.at[n], er.at[n], above[o]
                    )
                )

    ccol = lax.broadcasted_iota(jnp.int32, (tok_n, p.rows), 1).astype(F32)

    def combine(r):
        h = 0 if r in p.groups[0] else 1
        i = p.groups[h].index(r)
        total = jnp.zeros((tok_n, p.d), F32)
        for j in range(ny):
            pick = jnp.where(pcol[r, :, j : j + 1] + float(i * p.cap) == ccol, 1.0, 0.0).astype(BF16)
            rows = res[pl.ds(h * ny * p.rows, p.rows)] if j == 0 else rret[h * (ny - 1) + j - 1]
            total = total + pcol[r, :, 8 + j : 9 + j] * jnp.dot(pick, rows, preferred_element_type=F32)
        part[r] = total

    places(0)
    for s in range(2, p.half):
        ag_start(s)
        places(s - 1)
        places(nz - s + 1)
    ag_start(p.half)
    places(p.half - 1)
    places(nz - p.half + 1)
    dispatch(0)
    x_second()
    for way in (0, 1):
        agc[way, way, p.half].wait_recv()
    places(p.half)
    dispatch(1)
    x_third()
    x_ready()
    for h in (0, 1):
        for first in range(0, ny, 2):
            expert(h, first, min(2, ny - first))
    for h in (0, 1):
        for j in range(1, ny):
            ec[h, j].wait_recv()
        for r in sorted(p.groups[h], key=lambda r: -min(r, nz - r)):
            combine(r)

    rc = {}
    for way, half, dist in p.rs:
        n = p.rs.index((way, half, dist))
        first, size = p.rscut[half]
        off = dist if way == 0 else nz - dist
        total = part[off, pl.ds(first, size)]
        if (way, half, dist + 1) in rc:
            rc[way, half, dist + 1].wait_recv()
            total = total + rsin[p.rs.index((way, half, dist + 1)), pl.ds(0, size)].astype(F32)
        rsout[n, pl.ds(0, size)] = total.astype(BF16)
        rc[way, half, dist] = go(
            remote(
                rsout.at[n, pl.ds(0, size)],
                rsin.at[n, pl.ds(0, size)],
                rss.at[n],
                rsr.at[n],
                right if way == 0 else left,
            )
        )
    for half in (0, 1):
        first, size = p.rscut[half]
        total = part[0, pl.ds(first, size)]
        for way in (0, 1):
            rc[way, half, 1].wait_recv()
            total = total + rsin[p.rs.index((way, half, 1)), pl.ds(0, size)].astype(F32)
        out[pl.ds(first, size)] = total.astype(BF16)
    for copy in started:
        copy.wait_send()


def moe(p, tokx, weights):
    ny, nz, nx = p.ny, p.nz, p.nx
    dma = pltpu.SemaphoreType.DMA
    flat = weights
    return pl.pallas_call(
        functools.partial(moe_kernel, p),
        out_shape=jax.ShapeDtypeStruct((p.tok, p.d), BF16),
        in_specs=[pl.BlockSpec(memory_space=pltpu.VMEM), pl.BlockSpec(memory_space=pl.ANY)],
        out_specs=pl.BlockSpec(memory_space=pltpu.VMEM),
        scratch_shapes=[
            pltpu.VMEM((nz - 1, p.tok + META, p.d), BF16),
            pltpu.VMEM((2 * (ny - 1), p.rows, p.d), BF16),
            pltpu.VMEM((2 * ny * p.rows, p.d), BF16),
            pltpu.VMEM((nx, 2, 3, p.d, p.hs), BF16),
            pltpu.VMEM((2 * ny * p.rows, p.d), BF16),
            pltpu.VMEM((2 * (ny - 1), p.rows, p.d), BF16),
            pltpu.VMEM((nz, p.tok, p.d), F32),
            pltpu.VMEM((len(p.rs), p.tok // 2, p.d), BF16),
            pltpu.VMEM((len(p.rs), p.tok // 2, p.d), BF16),
            pltpu.VMEM((2 * p.rows, p.d), F32),
            pltpu.VMEM((nz, 8, p.tok), F32),
            pltpu.VMEM((nz, p.tok, 128), F32),
            dma((1,)),
            dma((len(p.ag),)),
            dma((len(p.ag),)),
            dma((8,)),
            dma((8,)),
            dma((2 * (ny - 1),)),
            dma((2 * (ny - 1),)),
            dma((2 * (ny - 1),)),
            dma((2 * (ny - 1),)),
            dma((len(p.rs),)),
            dma((len(p.rs),)),
        ],
        compiler_params=pltpu.CompilerParams(
            collective_id=0, has_side_effects=True, vmem_limit_bytes=60 * 1024 * 1024
        ),
        name="moe",
    )(tokx, flat)


def reorder(blocks, source_slot):
    n, rows, lanes = blocks.shape

    def copy(order, src, dst):
        dst[...] = src[...]

    return pl.pallas_call(
        copy,
        grid_spec=pltpu.PrefetchScalarGridSpec(
            num_scalar_prefetch=1,
            grid=(n,),
            in_specs=[pl.BlockSpec((1, rows, lanes), lambda s, order: (order[s], 0, 0))],
            out_specs=pl.BlockSpec((1, rows, lanes), lambda s, order: (s, 0, 0)),
        ),
        out_shape=jax.ShapeDtypeStruct(blocks.shape, blocks.dtype),
        name="reorder",
    )(source_slot, blocks)


def moves(weights, first_moment, second_moment, source_slot):
    n = lax.axis_size("expert")
    block = jnp.concatenate([weights, first_moment.astype(BF16), second_moment.astype(BF16)], axis=1)
    shape = block.shape
    block = block.reshape(n, -1, 128)
    spread = lax.all_to_all(block, "expert", split_axis=0, concat_axis=0, tiled=True)
    ordered = reorder(spread, source_slot)
    back = lax.all_to_all(ordered, "expert", split_axis=0, concat_axis=0, tiled=True).reshape(shape)
    me = lax.axis_index("expert")
    stays = source_slot[me] == me
    return (
        jnp.where(stays, weights, back[:, 0:3]),
        jnp.where(stays, first_moment, back[:, 3:6].astype(F32)),
        jnp.where(stays, second_moment, back[:, 6:9].astype(F32)),
    )


def per_device(n_y, tokens, route_ids, gate_weight, old_owner, new_owner, weights, first_moment, second_moment):
    n = lax.axis_size("expert")
    tok, d = tokens.shape
    p = Plan(lax.axis_size("dp"), n_y, n // n_y, tok, 3 * tok * route_ids.shape[1] // (2 * n), d, weights.shape[3])
    labels = jnp.arange(n, dtype=jnp.int32)
    source_slot = jnp.sum(jnp.where(new_owner[None, :] == labels[:, None], old_owner[None, :], 0), axis=1)
    slots = jnp.sum(jnp.where(route_ids[:, :, None] == labels, old_owner, 0), axis=2)
    high = lax.reduce_precision(gate_weight, 8, 7)
    meta = jnp.concatenate([slots.astype(F32), high, gate_weight - high, jnp.full((tok, META - 12), -1.0, F32)], axis=1)
    meta = jnp.pad(meta.T.astype(BF16), ((0, 0), (0, d - tok)))
    tokx = jnp.concatenate([tokens, meta], axis=0)
    layer_output = moe(p, tokx, weights[0])
    return (layer_output, *moves(weights, first_moment, second_moment, source_slot))


def solution(mesh):
    experts = mesh.shape["expert"]
    n_y = 4 if experts == 32 else 2
    placed = (
        P(("dp", "expert"), None),
        P(("dp", "expert"), None),
        P(("dp", "expert"), None),
        P(),
        P(),
        P("expert", None, None, "dp"),
        P("expert", None, None, "dp"),
        P("expert", None, None, "dp"),
    )
    return jax.shard_map(
        functools.partial(per_device, n_y),
        mesh=mesh,
        in_specs=placed,
        out_specs=(
            P(("dp", "expert"), None),
            P("expert", None, None, "dp"),
            P("expert", None, None, "dp"),
            P("expert", None, None, "dp"),
        ),
        check_vma=False,
    )
```

time: 436 us -> 276 us (0.63)
  waiting for transfers between devices: 255 us -> 57.1 us
  Pallas kernels: 0 us -> 186 us
  blocking collectives: 43.9 us -> 0 us
  local copies, waits for them, and re-layouts: 46.6 us -> 3.15 us
  starting transfers between devices: 44.1 us -> 15.8 us
  matrix products: 18.3 us -> 0 us
  between operations: 14.3 us -> 1.42 us
    all_to_all x7 -> x2, waiting for transfers between devices: 255 us -> 57.1 us  [the longest x1 57.1 us: moves(): lax.all_to_all(block, 'expert', split_axis=0, concat_axis=0, tiled=True)]
    pallas_call x0 -> x2, Pallas kernels: none -> 186 us  [the longest x1 169 us: moe(): pl.pallas_call(functools.partial(moe_kernel, p), out_shape=jax.ShapeDtype...]
    all_to_all x1 -> x0, blocking collectives: 43.9 us -> none  [relocate_moments(): lax.all_to_all(ordered[0], 'expert', split_axis=0, concat_axis=2, tiled=T...]
    all_to_all x7 -> x2, starting transfers between devices: 44.1 us -> 15.8 us  [the longest x1 11.6 us: moves(): lax.all_to_all(block, 'expert', split_axis=0, concat_axis=0, tiled=True)]
    dot_general x3 -> x0, matrix products: 18.3 us -> none  [the longest x1 10.2 us: per_device(): jnp.einsum('rh,dh->rd', hidden, shard_piece[0, 2], preferred_element_type...]
    gather x5 -> x0, local copies, waits for them, and re-layouts: 13.2 us -> none  [the longest x2 6.06 us: per_device(): jnp.take(returned, slot_index, axis=0).astype(jnp.float32)]
    reshape x4 -> x0, local copies, waits for them, and re-layouts: 11.1 us -> none  [the longest x1 4.08 us: per_device(): accumulated.astype(jnp.bfloat16)]
    all_to_all x6 -> x0, local copies, waits for them, and re-layouts: 11 us -> none  [the longest x1 2.94 us: relocate_moments(): lax.all_to_all(first_moment, 'expert', split_axis=2, concat_axis=0, tiled...]
  transfers between devices with their start and end apart: 8 -> 2, of which waited for: 7 -> 1; matrix products, arithmetic and copies ran while one was open for 14% -> 1% of each run, Pallas kernels for 0% -> 62%
where the time goes in v1:
time: 276 us; the launch traced here: 274 us
  Pallas kernels  186 us (67%)
  waiting for transfers between devices  57.1 us (21%)
  starting transfers between devices  15.8 us (6%)
  other arithmetic  9.9 us (4%)
  local copies, waits for them, and re-layouts  3.15 us (1%)
    pallas_call x1, Pallas kernels, moe(): pl.pallas_call(functools.partial(moe_kernel, p), out_shape=jax.ShapeDtype...  169 us
    all_to_all x1, waiting for transfers between devices, moves(): lax.all_to_all(block, 'expert', split_axis=0, concat_axis=0, tiled=True)  57.1 us
    pallas_call x1, Pallas kernels, reorder(): pl.pallas_call(copy, grid_spec=pltpu.PrefetchScalarGridSpec(num_scalar_pr...  17.8 us
    all_to_all x1, starting transfers between devices, moves(): lax.all_to_all(block, 'expert', split_axis=0, concat_axis=0, tiled=True)  11.6 us
  transfers between devices with their start and end apart: 2, of which 1 were waited for; matrix products, arithmetic and copies ran while one was open for 1% of the time, Pallas kernels for 62%

profile of v1, /device:TPU:2, one launch (start us, length us, event | category | flops | bytes accessed | tf_op | source)
XLA Modules:
  0.0 273.8 jit_solution(3280255872780610093)
XLA Ops:
  0.6 0.0 copy-start.3
  0.6 0.0 copy-start.1
  0.7 1.7 convert_element_type.23
  2.3 0.2 copy-done.3
  2.5 0.1 convert_element_type.24
  2.6 0.1 copy-done.1
  2.7 1.7 pad_maximum_fusion
  4.4 11.6 %all-to-all-start = ((bf16[32,288,128]{2,1,0:T(8,128)(2,1)}), bf16[32,288,128]{2,1,0:T(8,128)(2,1)S(1)}, u32[]{:S(2)}, u32[]{:S(2)}) async-start(bf16[32,288,128]{2,1,0:T(8,128)(2,1)} %bitcast.6), calls=%async_computation | async-start | bytes 4718592 | tf_op jit(solution)/shard_map/all_to_all | solution.py:390
  16.0 0.6 select_reduce_fusion.1.order
  16.7 57.1 %all-to-all-done.src = bf16[32,288,128]{2,1,0:T(8,128)(2,1)S(1)} async-done(((bf16[32,288,128]{2,1,0:T(8,128)(2,1)}), bf16[32,288,128]{2,1,0:T(8,128)(2,1)S(1)}, u32[]{:S(2)}, u32[]{:S(2)}) %all-to-all-start) | async-done | bytes 2359328 | tf_op jit(solution)/shard_map/all_to_all | solution.py:390
  73.8 1.4 copy-done
  75.2 17.8 %reorder.1 = bf16[32,288,128]{2,1,0:T(8,128)(2,1)} custom-call(s32[32]{0:T(128)} %select_reduce_fusion.1.order, bf16[32,288,128]{2,1,0:T(8,128)(2,1)} %copy-done), custom_call_target="tpu_custom_call" | custom-call | tf_op jit(solution)/shard_map/reorder/pallas_call | solution.py:372
  93.0 4.2 %all-to-all-start.1 = ((bf16[32,288,128]{2,1,0:T(8,128)(2,1)}), bf16[32,288,128]{2,1,0:T(8,128)(2,1)S(1)}, u32[]{:S(2)}, u32[]{:S(2)}) async-start(bf16[32,288,128]{2,1,0:T(8,128)(2,1)} %reorder.1), calls=%async_computation.1 | async-start | bytes 4718592 | tf_op jit(solution)/shard_map/all_to_all | solution.py:392
  97.2 0.6 dynamic_slice.3
  98.5 0.1 pad.13.clone
  98.6 0.1 select_reduce_fusion
  98.7 0.1 maximum_bitcast_fusion
  98.8 0.8 fusion.1.tokx
  99.5 168.6 %moe.1 = bf16[192,1024]{1,0:T(8,128)(2,1)} custom-call(bf16[208,1024]{1,0:T(8,128)(2,1)} %fusion.1.tokx, bf16[3,1024,128]{2,1,0:T(8,128)(2,1)} %bitcast.9), custom_call_target="tpu_custom_call" | custom-call | tf_op jit(solution)/shard_map/moe/pallas_call | solution.py:329
  268.1 0.0 copy-start.2
  268.2 3.9 %convert_select_fusion = (f32[1,3,1024,128]{3,2,1,0:T(8,128)}, f32[1,3,1024,128]{3,2,1,0:T(8,128)}) fusion(f32[1,3,1024,128]{3,2,1,0:T(8,128)} %param.15, bf16[1,9,1024,128]{3,2,1,0:T(8,128)(2,1)S(1)} %bitcast.7, pred[]{:T(512)S(6)} %eq.35, f32[1,3,1024,128]{3,2,1,0:T(8,128)} %param.14), kind=kLoop, calls=%fused_computation.1 | loop fusion | flops 1572864 | bytes 7864321 | tf_op jit(solution)/shard_map/jit(_where)/select_n | solution.py:398
  272.0 1.0 slice_select_fusion
  273.0 0.0 copy-done.4
  273.0 0.7 copy.14
  (19 shorter events, 0.0 us)
Async XLA Ops:
  0.6 1.9 copy-start.3
  0.6 2.1 copy-start.1
  4.4 11.6 %copy-start.9 = (s32[32]{0:T(128)S(1)}, s32[32]{0:T(128)}, u32[]{:S(2)}) copy-start(s32[32]{0:T(128)} %param.11) | copy-start | bytes 388
  4.4 11.6 %copy-start.10 = (s32[32]{0:T(128)S(1)}, s32[32]{0:T(128)}, u32[]{:S(2)}) copy-start(s32[32]{0:T(128)} %param.12) | copy-start | bytes 388
  4.4 69.4 %all-to-all-start = ((bf16[32,288,128]{2,1,0:T(8,128)(2,1)}), bf16[32,288,128]{2,1,0:T(8,128)(2,1)S(1)}, u32[]{:S(2)}, u32[]{:S(2)}) async-start(bf16[32,288,128]{2,1,0:T(8,128)(2,1)} %bitcast.6), calls=%async_computation | async-start | bytes 4718592 | tf_op jit(solution)/shard_map/all_to_all | solution.py:390
  73.8 1.4 copy-start
  93.0 4.2 %copy-start.8 = (s32[32]{0:T(128)S(1)}, s32[32]{0:T(128)}, u32[]{:S(2)}) copy-start(s32[32]{0:T(128)} %select_reduce_fusion.1.order) | copy-start | bytes 388
  93.0 5.6 %copy-start.6 = (s32[192,4]{0,1:T(4,128)S(1)}, s32[192,4]{0,1:T(4,128)}, u32[]{:S(2)}) copy-start(s32[192,4]{0,1:T(4,128)} %param.9) | copy-start | bytes 9220
  93.0 5.7 %copy-start.7 = (f32[192,4]{0,1:T(4,128)S(1)}, f32[192,4]{0,1:T(4,128)}, u32[]{:S(2)}) copy-start(f32[192,4]{0,1:T(4,128)} %param.10) | copy-start | bytes 9220
  93.0 5.8 %copy-start.5 = (bf16[192,1024]{1,0:T(8,128)(2,1)S(1)}, bf16[192,1024]{1,0:T(8,128)(2,1)}, u32[]{:S(2)}) copy-start(bf16[192,1024]{1,0:T(8,128)(2,1)} %param.8) | copy-start | bytes 1179652
  93.0 175.1 %all-to-all-start.1 = ((bf16[32,288,128]{2,1,0:T(8,128)(2,1)}), bf16[32,288,128]{2,1,0:T(8,128)(2,1)S(1)}, u32[]{:S(2)}, u32[]{:S(2)}) async-start(bf16[32,288,128]{2,1,0:T(8,128)(2,1)} %reorder.1), calls=%async_computation.1 | async-start | bytes 4718592 | tf_op jit(solution)/shard_map/all_to_all | solution.py:392
  268.1 3.9 %copy-start.2 = (bf16[1,3,1024,128]{3,2,1,0:T(8,128)(2,1)S(1)}, bf16[1,3,1024,128]{3,2,1,0:T(8,128)(2,1)}, u32[]{:S(2)}) copy-start(bf16[1,3,1024,128]{3,2,1,0:T(8,128)(2,1)} %param.13) | copy-start | bytes 2359300
  272.0 1.0 copy-start.4

commit v2 on v1

--- a/solution.py
+++ b/solution.py
@@ -25,6 +25,10 @@
         self.groups = (order[: self.half], order[self.half :])
         self.rows = self.half * cap
         self.yorder = [0, 1, 3, 2] if n_y == 4 else list(range(n_y))
+        self.chunks = 8
+        self.steps = self.chunks + self.half - 1
+        self.piece = 9 * d // n_y
+        self.chunk = self.piece // self.chunks
         cut = tok // 2
         self.agcut = ((0, cut), (cut, tok + META - cut))
         self.rscut = ((0, cut), (cut, tok - cut))
@@ -48,7 +52,10 @@
     p,
     tokx,
     wts,
+    block,
+    ctl,
     out,
+    moved,
     tokb,
     sendb,
     recvd,
@@ -61,6 +68,10 @@
     acc,
     prow,
     pcol,
+    spread,
+    cin,
+    cout,
+    fin,
     lsem,
     ags,
     agr,
@@ -72,6 +83,12 @@
     er,
     rss,
     rsr,
+    ss,
+    sr,
+    cs,
+    cr,
+    fs,
+    fr,
 ):
     ny, nz, nx = p.ny, p.nz, p.nx
     dp = lax.axis_index("dp")
@@ -141,6 +158,81 @@
     if nx > 1:
         xc.append(go(remote(wts, wall.at[3, 0], xs.at[1], xr.at[1], xright)))
         xc.append(go(remote(wts, wall.at[1, 0], xs.at[2], xr.at[2], xleft)))
+
+    keep_piece = pltpu.make_async_copy(block.at[y], spread.at[y], lsem.at[1])
+    keep_piece.start()
+    sc = [
+        go(remote(block.at[(y + j) % ny], spread.at[y], ss.at[j - 1], sr.at[j - 1], above[j]))
+        for j in range(1, ny)
+    ]
+
+    def spread_ready():
+        keep_piece.wait()
+        for copy in sc:
+            copy.wait_recv()
+
+    cc = {}
+
+    def convey(t):
+        for lane in (0, 1):
+            for way in (0, 1):
+                n = (way * 2 + lane) * p.steps + t
+                c = (way * 2 + lane) * 3
+                if t > 0:
+                    for inlane in (0, 1):
+                        if (way, inlane, t - 1) not in arrived:
+                            cc[way, inlane, t - 1].wait_recv()
+                            arrived.add((way, inlane, t - 1))
+                    value = jnp.where(
+                        ctl[c + 2] == 1, cin[(way * 2 + 1) * p.steps + t - 1], cin[way * 2 * p.steps + t - 1]
+                    )
+                    if t < p.chunks:
+                        value = jnp.where(ctl[c] == 1, spread[ctl[c + 1], pl.ds(t * p.chunk, p.chunk)], value)
+                else:
+                    value = spread[ctl[c + 1], pl.ds(0, p.chunk)]
+                cout[n] = value
+                cc[way, lane, t] = go(
+                    remote(cout.at[n], cin.at[n], cs.at[n], cr.at[n], right if way == 0 else left)
+                )
+
+    arrived = set()
+    todo = list(range(p.steps))
+
+    def convey_next(count=1):
+        for _ in range(count):
+            if todo:
+                convey(todo.pop(0))
+
+    fc = []
+
+    def deliver():
+        for way in (0, 1):
+            for lane in (0, 1):
+                cc[way, lane, p.steps - 1].wait_recv()
+        for j in list(range(1, ny)) + [0]:
+            c = 12 + ((y + j) % ny) * 4
+            kind, ysrc, lane, skew = ctl[c], ctl[c + 1], ctl[c + 2], ctl[c + 3]
+            from_cw = lane * p.steps + skew
+            from_ccw = (2 + lane) * p.steps + skew
+
+            def one(k, carry):
+                rows = pl.ds(pl.multiple_of(k * p.chunk, p.chunk), p.chunk)
+                value = jnp.where(kind == 1, cin[from_cw + k], cin[from_ccw + k])
+                fin[j, rows] = jnp.where(kind == 0, spread[ysrc, rows], value)
+                return carry
+
+            lax.fori_loop(0, p.chunks, one, 0)
+            if j == 0:
+                own = pltpu.make_async_copy(fin.at[0], moved.at[y], lsem.at[2])
+                own.start()
+                fc.append(own)
+            else:
+                fc.append(go(remote(fin.at[j], moved.at[y], fs.at[j - 1], fr.at[j - 1], above[j])))
+
+    def delivered():
+        for copy in fc[:-1]:
+            copy.wait_recv()
+        fc[-1].wait()
 
     def x_second():
         if nx > 1:
@@ -277,20 +369,27 @@
     places(nz - p.half + 1)
     dispatch(0)
     x_second()
+    spread_ready()
     for way in (0, 1):
         agc[way, way, p.half].wait_recv()
     places(p.half)
+    convey_next()
     dispatch(1)
+    convey_next()
     x_third()
     x_ready()
     for h in (0, 1):
         for first in range(0, ny, 2):
             expert(h, first, min(2, ny - first))
+            convey_next()
     for h in (0, 1):
         for j in range(1, ny):
             ec[h, j].wait_recv()
         for r in sorted(p.groups[h], key=lambda r: -min(r, nz - r)):
             combine(r)
+            convey_next()
+    convey_next(len(todo))
+    deliver()
 
     rc = {}
     for way, half, dist in p.rs:
@@ -318,19 +417,27 @@
             rc[way, half, 1].wait_recv()
             total = total + rsin[p.rs.index((way, half, 1)), pl.ds(0, size)].astype(F32)
         out[pl.ds(first, size)] = total.astype(BF16)
+    delivered()
     for copy in started:
         copy.wait_send()
 
 
-def moe(p, tokx, weights):
+def moe(p, tokx, weights, block, ctl):
     ny, nz, nx = p.ny, p.nz, p.nx
     dma = pltpu.SemaphoreType.DMA
-    flat = weights
     return pl.pallas_call(
         functools.partial(moe_kernel, p),
-        out_shape=jax.ShapeDtypeStruct((p.tok, p.d), BF16),
-        in_specs=[pl.BlockSpec(memory_space=pltpu.VMEM), pl.BlockSpec(memory_space=pl.ANY)],
-        out_specs=pl.BlockSpec(memory_space=pltpu.VMEM),
+        out_shape=(
+            jax.ShapeDtypeStruct((p.tok, p.d), BF16),
+            jax.ShapeDtypeStruct((ny, p.piece, p.hs), BF16),
+        ),
+        in_specs=[
+            pl.BlockSpec(memory_space=pltpu.VMEM),
+            pl.BlockSpec(memory_space=pl.ANY),
+            pl.BlockSpec(memory_space=pl.ANY),
+            pl.BlockSpec(memory_space=pltpu.SMEM),
+        ],
+        out_specs=(pl.BlockSpec(memory_space=pltpu.VMEM), pl.BlockSpec(memory_space=pl.ANY)),
         scratch_shapes=[
             pltpu.VMEM((nz - 1, p.tok + META, p.d), BF16),
             pltpu.VMEM((2 * (ny - 1), p.rows, p.d), BF16),
@@ -344,7 +451,11 @@
             pltpu.VMEM((2 * p.rows, p.d), F32),
             pltpu.VMEM((nz, 8, p.tok), F32),
             pltpu.VMEM((nz, p.tok, 128), F32),
-            dma((1,)),
+            pltpu.VMEM((ny, p.piece, p.hs), BF16),
+            pltpu.VMEM((4 * p.steps, p.chunk, p.hs), BF16),
+            pltpu.VMEM((4 * p.steps, p.chunk, p.hs), BF16),
+            pltpu.VMEM((ny, p.piece, p.hs), BF16),
+            dma((3,)),
             dma((len(p.ag),)),
             dma((len(p.ag),)),
             dma((8,)),
@@ -355,48 +466,52 @@
             dma((2 * (ny - 1),)),
             dma((len(p.rs),)),
             dma((len(p.rs),)),
+            dma((ny - 1,)),
+            dma((ny - 1,)),
+            dma((4 * p.steps,)),
+            dma((4 * p.steps,)),
+            dma((ny - 1,)),
+            dma((ny - 1,)),
         ],
         compiler_params=pltpu.CompilerParams(
             collective_id=0, has_side_effects=True, vmem_limit_bytes=60 * 1024 * 1024
         ),
         name="moe",
-    )(tokx, flat)
-
-
-def reorder(blocks, source_slot):
-    n, rows, lanes = blocks.shape
-
-    def copy(order, src, dst):
-        dst[...] = src[...]
-
-    return pl.pallas_call(
-        copy,
-        grid_spec=pltpu.PrefetchScalarGridSpec(
-            num_scalar_prefetch=1,
-            grid=(n,),
-            in_specs=[pl.BlockSpec((1, rows, lanes), lambda s, order: (order[s], 0, 0))],
-            out_specs=pl.BlockSpec((1, rows, lanes), lambda s, order: (s, 0, 0)),
-        ),
-        out_shape=jax.ShapeDtypeStruct(blocks.shape, blocks.dtype),
-        name="reorder",
-    )(source_slot, blocks)
-
-
-def moves(weights, first_moment, second_moment, source_slot):
-    n = lax.axis_size("expert")
-    block = jnp.concatenate([weights, first_moment.astype(BF16), second_moment.astype(BF16)], axis=1)
-    shape = block.shape
-    block = block.reshape(n, -1, 128)
-    spread = lax.all_to_all(block, "expert", split_axis=0, concat_axis=0, tiled=True)
-    ordered = reorder(spread, source_slot)
-    back = lax.all_to_all(ordered, "expert", split_axis=0, concat_axis=0, tiled=True).reshape(shape)
-    me = lax.axis_index("expert")
-    stays = source_slot[me] == me
-    return (
-        jnp.where(stays, weights, back[:, 0:3]),
-        jnp.where(stays, first_moment, back[:, 3:6].astype(F32)),
-        jnp.where(stays, second_moment, back[:, 6:9].astype(F32)),
-    )
+    )(tokx, weights, block, ctl)
+
+
+def routes(p, source_slot):
+    nz = p.nz
+    ex = lax.axis_index("expert")
+    z = ex % nz
+    slot = jnp.arange(p.ny * nz, dtype=jnp.int32)
+    zs, ys, zd = source_slot % nz, source_slot // nz, slot % nz
+    ahead = (zd - zs + nz) % nz
+    far = (ahead, (nz - ahead) % nz)
+    goes = ((ahead >= 1) & (ahead <= p.half), ahead > p.half)
+    earlier = slot[None, :] < slot[:, None]
+
+    def lanes(way, at):
+        passed = (at - zs + 2 * nz) % nz if way == 0 else (zs - at + 2 * nz) % nz
+        on = goes[way] & (passed < far[way])
+        return on, jnp.sum((earlier & on[None, :]).astype(jnp.int32), axis=1)
+
+    numbers = []
+    into = []
+    for way in (0, 1):
+        on_out, lane_out = lanes(way, z)
+        _, lane_in = lanes(way, z - 1 if way == 0 else z + 1)
+        into.append(lane_in)
+        for lane in (0, 1):
+            this = on_out & (lane_out == lane)
+            for what in ((zs == z).astype(jnp.int32), ys, lane_in):
+                numbers.append(jnp.sum(jnp.where(this, what, 0)))
+    kind = jnp.where(goes[0], 1, jnp.where(goes[1], 2, 0))
+    lane = jnp.where(goes[0], into[0], jnp.where(goes[1], into[1], 0))
+    skew = jnp.where(goes[0], far[0] - 1, jnp.where(goes[1], far[1] - 1, 0))
+    table = jnp.stack([kind, ys, lane, skew], axis=1).reshape(p.ny, nz, 4)
+    mine = jnp.sum(jnp.where((jnp.arange(nz) == z)[None, :, None], table, 0), axis=1)
+    return jnp.concatenate([jnp.stack(numbers), mine.reshape(-1)]).astype(jnp.int32)
 
 
 def per_device(n_y, tokens, route_ids, gate_weight, old_owner, new_owner, weights, first_moment, second_moment):
@@ -410,8 +525,19 @@
     meta = jnp.concatenate([slots.astype(F32), high, gate_weight - high, jnp.full((tok, META - 12), -1.0, F32)], axis=1)
     meta = jnp.pad(meta.T.astype(BF16), ((0, 0), (0, d - tok)))
     tokx = jnp.concatenate([tokens, meta], axis=0)
-    layer_output = moe(p, tokx, weights[0])
-    return (layer_output, *moves(weights, first_moment, second_moment, source_slot))
+    block = jnp.concatenate([weights[0], first_moment[0].astype(BF16), second_moment[0].astype(BF16)], axis=0)
+    layer_output, moved = moe(
+        p, tokx, weights[0], block.reshape(p.ny, p.piece, p.hs), routes(p, source_slot)
+    )
+    moved = moved.reshape((1, *block.shape))
+    me = lax.axis_index("expert")
+    stays = jnp.sum(jnp.where(labels == me, source_slot, 0)) == me
+    return (
+        layer_output,
+        jnp.where(stays, weights, moved[:, 0:3]),
+        jnp.where(stays, first_moment, moved[:, 3:6].astype(F32)),
+        jnp.where(stays, second_moment, moved[:, 6:9].astype(F32)),
+    )
 
 
 def solution(mesh):

time: 276 us -> 170 us (0.62)
  waiting for transfers between devices: 57.1 us -> 0 us
  Pallas kernels: 186 us -> 142 us
  starting transfers between devices: 15.8 us -> 0 us
  local copies, waits for them, and re-layouts: 3.15 us -> 9.48 us
  other arithmetic: 9.9 us -> 15.8 us
    all_to_all x2 -> x0, waiting for transfers between devices: 57.1 us -> none  [the longest x1 57.1 us: moves(): lax.all_to_all(block, 'expert', split_axis=0, concat_axis=0, tiled=True)]
    pallas_call x2 -> x1, Pallas kernels: 186 us -> 142 us  [moe(): pl.pallas_call(functools.partial(moe_kernel, p), out_shape=(jax.ShapeDtyp...]
    all_to_all x2 -> x0, starting transfers between devices: 15.8 us -> none  [the longest x1 11.6 us: moves(): lax.all_to_all(block, 'expert', split_axis=0, concat_axis=0, tiled=True)]
    concatenate x0 -> x1, local copies, waits for them, and re-layouts: none -> 8.21 us  [routes(): jnp.concatenate([jnp.stack(numbers), mine.reshape(-1)]).astype(jnp.int32)]
    select_n x2 -> x4, other arithmetic: 4.87 us -> 5.66 us  [the longest x1 3.41 us: per_device(): jnp.where(stays, second_moment, moved[:, 6:9].astype(F32))]
  transfers between devices with their start and end apart: 2 -> 0, of which waited for: 1 -> 0; matrix products, arithmetic and copies ran while one was open for 1% -> 0% of each run, Pallas kernels for 62% -> 0%
where the time goes in v2:
time: 170 us; the launch traced here: 169 us
  Pallas kernels  142 us (84%)
  other arithmetic  15.8 us (9%)
  local copies, waits for them, and re-layouts  9.48 us (6%)
    pallas_call x1, Pallas kernels, moe(): pl.pallas_call(functools.partial(moe_kernel, p), out_shape=(jax.ShapeDtyp...  142 us
    concatenate x1, local copies, waits for them, and re-layouts, routes(): jnp.concatenate([jnp.stack(numbers), mine.reshape(-1)]).astype(jnp.int32)  8.21 us
    select_n x1, other arithmetic, per_device(): jnp.where(stays, second_moment, moved[:, 6:9].astype(F32))  3.41 us

profile of v2, /device:TPU:2, one launch (start us, length us, event | category | flops | bytes accessed | tf_op | source)
XLA Modules:
  0.0 168.6 jit_solution(11707004358284390996)
XLA Ops:
  0.6 0.8 select_reduce_fusion.1
  1.4 0.1 pad.17.clone
  1.6 0.1 convert_reduce_fusion
  1.7 0.1 convert_reduce_fusion.3
  1.8 0.1 convert_reduce_fusion.1
  1.9 0.1 reduce_sum.206
  2.0 0.1 reduce_sum.205
  2.1 0.1 reduce_sum.204
  2.2 0.8 select_reduce_fusion.2
  3.6 0.8 select_reduce_fusion.8
  4.4 0.8 select_reduce_fusion
  5.3 0.1 fusion.6
  5.4 0.1 copy.15
  5.5 0.1 reshape.459
  5.6 8.2 %concatenate.17.ctl = s32[28]{0:T(128)} concatenate(s32[1]{0:T(128)} %bitcast.5, s32[1]{0:T(128)} %bitcast.6, s32[1]{0:T(128)} %bitcast.7, s32[1]{0:T(128)} %bitcast.8, s32[1]{0:T(128)} %bitcast.9, s32[1]{0:T(128)} %bitcast.10, s32[1]{0:T(128)} %bitcast.11, s32[1]{0:T(128)} %bitcast.12, s32[1]{0:T(128)} %bitcast.13, s32[1]{0:T(128)} %bitcast.14, s32[1]{0:T(128)} %bitcast.15, ...), dimensions={0} | concatenate | bytes 224 | tf_op jit(solution)/shard_map/concatenate | solution.py:514
  13.8 0.7 reduce-precision_convert_fusion
  14.5 0.1 maximum_bitcast_fusion
  14.6 1.8 %fusion.1.tokx = bf16[208,1024]{1,0:T(8,128)(2,1)} fusion(bf16[16,192]{1,0:T(8,128)(2,1)S(1)} %maximum_bitcast_fusion, bf16[192,1024]{1,0:T(8,128)(2,1)} %param.8), kind=kLoop, calls=%fused_computation.8 | loop fusion | flops 1277952 | bytes 825344 | tf_op jit(solution)/shard_map/concatenate | solution.py:527
  16.4 2.2 %convert_bitcast_fusion = (bf16[3,1024,128]{2,1,0:T(8,128)(2,1)S(1)}, bf16[3,1024,128]{2,1,0:T(8,128)(2,1)S(1)}) fusion(f32[1,3,1024,128]{3,2,1,0:T(8,128)} %param.15, f32[1,3,1024,128]{3,2,1,0:T(8,128)} %param.14), kind=kLoop, calls=%fused_computation.6 | loop fusion | flops 786432 | bytes 4718592 | tf_op jit(solution)/shard_map/convert_element_type | solution.py:528
  18.5 1.7 pad_maximum_fusion
  20.2 142.0 %moe.1 = (bf16[192,1024]{1,0:T(8,128)(2,1)}, bf16[4,2304,128]{2,1,0:T(8,128)(2,1)}) custom-call(bf16[208,1024]{1,0:T(8,128)(2,1)} %fusion.1.tokx, bf16[3,1024,128]{2,1,0:T(8,128)(2,1)} %bitcast.22, bf16[4,2304,128]{2,1,0:T(8,128)(2,1)} %bitcast.21, s32[28]{0:T(128)} %concatenate.17.ctl), custom_call_target="tpu_custom_call" | custom-call | tf_op jit(solution)/shard_map/moe/pallas_call | solution.py:428
  162.3 2.2 %slice_select_fusion = bf16[1,3,1024,128]{3,2,1,0:T(8,128)(2,1)} fusion(bf16[1,3,1024,128]{3,2,1,0:T(8,128)(2,1)S(1)} %copy-done.1, bf16[1,9,1024,128]{3,2,1,0:T(8,128)(2,1)} %bitcast.24, pred[]{:T(512)S(6)} %eq.102), kind=kLoop, calls=%fused_computation.5 | loop fusion | flops 393216 | bytes 2359297 | tf_op jit(solution)/shard_map/jit(_where)/select_n | solution.py:537
  164.5 3.4 %convert_select_fusion = (f32[1,3,1024,128]{3,2,1,0:T(8,128)}, f32[1,3,1024,128]{3,2,1,0:T(8,128)}) fusion(f32[1,3,1024,128]{3,2,1,0:T(8,128)S(1)} %copy-done.2, bf16[1,9,1024,128]{3,2,1,0:T(8,128)(2,1)} %bitcast.25, pred[]{:T(512)S(6)} %eq.102, f32[1,3,1024,128]{3,2,1,0:T(8,128)S(1)} %copy-done.3), kind=kLoop, calls=%fused_computation.1 | loop fusion | flops 1572864 | bytes 7864321 | tf_op jit(solution)/shard_map/jit(_where)/select_n | solution.py:539
  167.9 0.7 copy.17
  (17 shorter events, 0.1 us)
Async XLA Ops:
  16.4 2.2 %copy-start = (bf16[1,3,1024,128]{3,2,1,0:T(8,128)(2,1)S(1)}, bf16[1,3,1024,128]{3,2,1,0:T(8,128)(2,1)}, u32[]{:S(2)}) copy-start(bf16[1,3,1024,128]{3,2,1,0:T(8,128)(2,1)} %param.13) | copy-start | bytes 2359300
  20.2 142.0 %copy-start.1 = (bf16[1,3,1024,128]{3,2,1,0:T(8,128)(2,1)S(1)}, bf16[1,3,1024,128]{3,2,1,0:T(8,128)(2,1)}, u32[]{:S(2)}) copy-start(bf16[1,3,1024,128]{3,2,1,0:T(8,128)(2,1)} %param.13) | copy-start | bytes 2359300
  20.2 144.3 %copy-start.3 = (f32[1,3,1024,128]{3,2,1,0:T(8,128)S(1)}, f32[1,3,1024,128]{3,2,1,0:T(8,128)}, u32[]{:S(2)}) copy-start(f32[1,3,1024,128]{3,2,1,0:T(8,128)} %param.14) | copy-start | bytes 4718596
  162.2 2.2 %copy-start.2 = (f32[1,3,1024,128]{3,2,1,0:T(8,128)S(1)}, f32[1,3,1024,128]{3,2,1,0:T(8,128)}, u32[]{:S(2)}) copy-start(f32[1,3,1024,128]{3,2,1,0:T(8,128)} %param.15) | copy-start | bytes 4718596
  164.5 3.4 %copy-start.4 = (bf16[192,1024]{1,0:T(8,128)(2,1)S(1)}, bf16[192,1024]{1,0:T(8,128)(2,1)}, u32[]{:S(2)}) copy-start(bf16[192,1024]{1,0:T(8,128)(2,1)} %get-tuple-element.54) | copy-start | bytes 1179652

commit v3 on v1

v3 whole, which is shorter than its diff:
```python
import functools

import jax
import jax.numpy as jnp
from jax import lax
from jax.experimental import pallas as pl
from jax.experimental.pallas import tpu as pltpu
from jax.sharding import PartitionSpec as P

MESH = pl.DeviceIdType.MESH
F32 = jnp.float32
BF16 = jnp.bfloat16
META = 16


class Plan:
    def __init__(self, n_dp, n_y, n_z, tok, cap, d, hs):
        self.nx, self.ny, self.nz = n_dp // 2, n_y, n_z
        self.tok, self.cap, self.d, self.hs = tok, cap, d, hs
        self.half = n_z // 2
        order = [0]
        for s in range(1, self.half):
            order += [s, n_z - s]
        order += [self.half]
        self.groups = (order[: self.half], order[self.half :])
        self.rows = self.half * cap
        self.yorder = [0, 1, 3, 2] if n_y == 4 else list(range(n_y))
        self.chunks = 8
        self.steps = self.chunks + self.half - 1
        self.piece = 9 * d // n_y
        self.chunk = self.piece // self.chunks
        cut = tok // 2
        self.agcut = ((0, cut), (cut, tok + META - cut))
        self.rscut = ((0, cut), (cut, tok - cut))
        self.ag = [
            (way, part, s)
            for s in range(1, self.half + 1)
            for way in (0, 1)
            for part in (0, 1)
            if s < self.half or way == part
        ]
        self.rs = [
            (way, part, dist)
            for dist in range(self.half, 0, -1)
            for way in (0, 1)
            for part in (0, 1)
            if dist < self.half or way == part
        ]


class Link:
    def __init__(self, src, dst, send, recv, to):
        self.copy = pltpu.make_async_remote_copy(
            src_ref=src, dst_ref=dst, send_sem=send, recv_sem=recv, device_id=to, device_id_type=MESH
        )
        self.copy.start()
        self.here = False

    def arrive(self):
        if not self.here:
            self.copy.wait_recv()
            self.here = True


def moe_kernel(
    p,
    tokens,
    route,
    gate,
    old,
    new,
    wts,
    first_m,
    second_m,
    out,
    moved,
    tokb,
    sendb,
    recvd,
    wall,
    res,
    rret,
    part,
    rsin,
    rsout,
    acc,
    prow,
    pcol,
    stage,
    block,
    spread,
    cin,
    cout,
    fin,
    lsem,
    ags,
    agr,
    xs,
    xr,
    ds,
    dr,
    es,
    er,
    rss,
    rsr,
    ss,
    sr,
    cs,
    cr,
    fs,
    fr,
):
    ny, nz, nx = p.ny, p.nz, p.nx
    tok_n = p.tok
    dp = lax.axis_index("dp")
    ex = lax.axis_index("expert")
    x, core = dp // 2, dp % 2
    y, z = ex // nz, ex % nz
    right = (dp, y * nz + (z + 1) % nz)
    left = (dp, y * nz + (z + nz - 1) % nz)
    along = (right, left)
    above = [None] + [(dp, ((y + j) % ny) * nz + z) for j in range(1, ny)]
    twin = (x * 2 + 1 - core, ex)
    xright = (((x + 1) % nx) * 2 + core, ex)
    xleft = (((x + nx - 1) % nx) * 2 + core, ex)
    started = []

    def go(*what):
        link = Link(*what)
        started.append(link)
        return link

    def local(n, src, dst):
        copy = pltpu.make_async_copy(src, dst, lsem.at[n])
        copy.start()
        return copy

    own_tokens = local(0, tokens, tokb.at[0, pl.ds(0, tok_n)])
    own_weights = local(1, wts, wall.at[0, 0])
    wrows = 3 * p.d
    block_weights = local(2, wts, block.at[pl.ds(0, wrows)])
    stage_first = local(3, first_m, stage.at[0])
    stage_second = local(4, second_m, stage.at[1])

    barrier = pltpu.get_barrier_semaphore()
    peers = [right, left, twin] + above[1:] + ([xright, xleft] if nx > 1 else [])
    for peer in peers:
        pl.semaphore_signal(barrier, inc=1, device_id=peer, device_id_type=MESH)
    pl.semaphore_wait(barrier, len(peers))

    agc = {}

    def ag_send(way, half, s):
        src = (nz - (s - 1)) % nz if way == 0 else s - 1
        dst = nz - s if way == 0 else s
        rows = pl.ds(*p.agcut[half])
        n = p.ag.index((way, half, s))
        source = tokens.at[rows] if (s, half) == (1, 0) else tokb.at[src, rows]
        agc[way, half, s] = go(source, tokb.at[dst, rows], ags.at[n], agr.at[n], along[way])

    def ag_step(s):
        for way, half, step in p.ag:
            if step == s:
                agc[way, half, s - 1].arrive()
                ag_send(way, half, s)
        for way, half, step in p.ag:
            if step == s - 1:
                agc[way, half, step].arrive()

    for way in (0, 1):
        ag_send(way, 0, 1)

    xc = [go(wts, wall.at[0, 1], xs.at[0], xr.at[0], twin)]
    if nx > 1:
        xc.append(go(wts, wall.at[3, 0], xs.at[1], xr.at[1], xright))
        xc.append(go(wts, wall.at[1, 0], xs.at[2], xr.at[2], xleft))

    def x_second():
        if nx > 1:
            lo, hi = pl.ds(0, wrows // 2), pl.ds(wrows // 2, wrows // 2)
            xc[1].arrive()
            xc.append(go(wall.at[3, 0, lo], wall.at[2, 0, lo], xs.at[3], xr.at[3], xright))
            xc.append(go(wall.at[3, 0], wall.at[3, 1], xs.at[4], xr.at[4], twin))
            xc[2].arrive()
            xc.append(go(wall.at[1, 0, hi], wall.at[2, 0, hi], xs.at[5], xr.at[5], xleft))
            xc.append(go(wall.at[1, 0], wall.at[1, 1], xs.at[6], xr.at[6], twin))

    def x_third():
        if nx > 1:
            xc[3].arrive()
            xc[5].arrive()
            xc.append(go(wall.at[2, 0], wall.at[2, 1], xs.at[7], xr.at[7], twin))

    def x_ready():
        own_weights.wait()
        for link in xc:
            link.arrive()

    slots = jnp.zeros((4, tok_n), jnp.int32)
    for e in range(ny * nz):
        slots = jnp.where(route[...] == e, old[e], slots)
    g = gate[...]
    high = g.astype(BF16).astype(F32)
    meta = jnp.concatenate([slots.astype(F32), high, g - high, jnp.full((4, tok_n), -1.0, F32)], axis=0)
    wide = -(-tok_n // 128) * 128
    if wide > tok_n:
        meta = jnp.concatenate([meta, jnp.zeros((META, wide - tok_n), F32)], axis=1)
    tokb[0, pl.ds(tok_n, META), pl.ds(0, wide)] = meta.astype(BF16)
    if wide < p.d:
        tokb[0, pl.ds(tok_n, META), pl.ds(wide, p.d - wide)] = jnp.zeros((META, p.d - wide), BF16)
    own_tokens.wait()
    for way in (0, 1):
        ag_send(way, 1, 1)

    block_weights.wait()
    stage_first.wait()
    stage_second.wait()
    step_rows = 256

    def narrow(i, carry):
        for a in (0, 1):
            rows = pl.ds(pl.multiple_of(i * step_rows, step_rows), step_rows)
            to = pl.ds(pl.multiple_of((1 + a) * wrows + i * step_rows, step_rows), step_rows)
            block[to] = stage[a, rows].astype(BF16)
        return carry

    lax.fori_loop(0, wrows // step_rows, narrow, 0)

    def piece(i):
        return block.at[pl.ds(pl.multiple_of(i * p.piece, p.piece), p.piece)]

    keep_piece = local(5, piece(y), spread.at[y])
    sc = [go(piece((y + j) % ny), spread.at[y], ss.at[j - 1], sr.at[j - 1], above[j]) for j in range(1, ny)]

    def spread_ready():
        keep_piece.wait()
        for link in sc:
            link.arrive()

    def scan(e, carry):
        seen, named = carry
        zs, zd = old[e] % nz, new[e] % nz
        ahead = (zd - zs + nz) % nz
        seen = list(seen)
        for way in (0, 1):
            goes = (ahead >= 1) & (ahead <= p.half) if way == 0 else ahead > p.half
            far = ahead if way == 0 else nz - ahead
            for into in (0, 1):
                at = z + nz - into if way == 0 else z + into
                passed = (at - zs + nz) % nz if way == 0 else (zs - at + 2 * nz) % nz
                on = goes & (passed < far)
                n = (way * 2 + into) * 2
                seen[n] = jnp.where(on & (seen[n] < 0), e, seen[n])
                seen[n + 1] = jnp.where(on, e, seen[n + 1])
        named = tuple(jnp.where(new[e] == yy * nz + z, e, named[yy]) for yy in range(ny))
        return tuple(seen), named

    none = jnp.int32(-1)
    seen, named = lax.fori_loop(0, ny * nz, scan, ((none,) * 8, (none,) * ny))
    lanes = {}
    for way in (0, 1):
        for lane in (0, 1):
            e = jnp.maximum(seen[way * 4 + lane], 0)
            lanes[way, lane] = (old[e] % nz == z, old[e] // nz, e != seen[way * 4 + 2])
    finals = []
    for yy in range(ny):
        e = jnp.maximum(named[yy], 0)
        ahead = (new[e] % nz - old[e] % nz + nz) % nz
        by_cw = ahead <= p.half
        lane = jnp.where(e != jnp.where(by_cw, seen[2], seen[6]), 1, 0)
        skew = jnp.maximum(jnp.where(by_cw, ahead, nz - ahead) - 1, 0)
        finals.append((ahead == 0, by_cw, old[e] // nz, lane * p.steps + skew))

    cc = {}
    todo = list(range(p.steps))

    def convey(t):
        for lane in (0, 1):
            for way in (0, 1):
                n = (way * 2 + lane) * p.steps + t
                mine, ysrc, second = lanes[way, lane]
                if t > 0:
                    for inlane in (0, 1):
                        cc[way, inlane, t - 1].arrive()
                    value = jnp.where(second, cin[(way * 2 + 1) * p.steps + t - 1], cin[way * 2 * p.steps + t - 1])
                    if t < p.chunks:
                        value = jnp.where(mine, spread[ysrc, pl.ds(t * p.chunk, p.chunk)], value)
                else:
                    value = spread[ysrc, pl.ds(0, p.chunk)]
                cout[n] = value
                cc[way, lane, t] = go(cout.at[n], cin.at[n], cs.at[n], cr.at[n], along[way])

    def convey_next(count=1):
        for _ in range(count):
            if todo:
                convey(todo.pop(0))

    def choose(ny_first):
        for way in (0, 1):
            for lane in (0, 1):
                cc[way, lane, p.steps - 1].arrive()
        for j in ny_first:
            stay, by_cw, ysrc, at = finals[0]
            for yy in range(1, ny):
                here = (y + j) % ny == yy
                other = finals[yy]
                stay = (here & other[0]) | (~here & stay)
                by_cw = (here & other[1]) | (~here & by_cw)
                ysrc = jnp.where(here, other[2], ysrc)
                at = jnp.where(here, other[3], at)

            def one(k, carry):
                rows = pl.ds(pl.multiple_of(k * p.chunk, p.chunk), p.chunk)
                value = jnp.where(by_cw, cin[at + k], cin[2 * p.steps + at + k])
                fin[j, rows] = jnp.where(stay, spread[ysrc, rows], value)
                return carry

            lax.fori_loop(0, p.chunks, one, 0)

    fc = []

    def deliver():
        for j in range(1, ny):
            fc.append(go(fin.at[j], moved.at[y], fs.at[j - 1], fr.at[j - 1], above[j]))
        fc.append(local(6, fin.at[0], moved.at[y]))

    ta = lax.broadcasted_iota(jnp.int32, (tok_n, tok_n), 0)
    tb = lax.broadcasted_iota(jnp.int32, (tok_n, tok_n), 1)
    before = (ta < tb).astype(F32).astype(BF16)
    after = (tb < ta).astype(F32).astype(BF16)
    same = (ta == tb).astype(F32).astype(BF16)
    jrow = lax.broadcasted_iota(jnp.int32, (8, 1), 0)
    yrow = jnp.where(jrow + y >= ny, jrow + y - ny, jrow + y)
    column = jnp.where(jrow < ny, yrow * nz + z, -5).astype(F32)
    nt = (((1,), (1,)), ((), ()))

    def places(r):
        m = tokb[r, pl.ds(tok_n, META), pl.ds(0, tok_n)].astype(F32)
        named = jnp.zeros((8, tok_n), F32)
        ghi = jnp.zeros((8, tok_n), F32)
        glo = jnp.zeros((8, tok_n), F32)
        for k in range(4):
            hit = m[k : k + 1] == column
            named = named + jnp.where(hit, 1.0, 0.0)
            ghi = ghi + jnp.where(hit, m[4 + k : 5 + k], 0.0)
            glo = glo + jnp.where(hit, m[8 + k : 9 + k], 0.0)
        nb = named.astype(BF16)
        rank = jnp.dot(nb, before, preferred_element_type=F32)
        prow[r] = jnp.where(named > 0.5, rank, -4096.0)
        rank_c = lax.dot_general(after, nb, nt, preferred_element_type=F32)
        named_c = lax.dot_general(same, nb, nt, preferred_element_type=F32)
        gate_c = lax.dot_general(same, ghi.astype(BF16), nt, preferred_element_type=F32) + lax.dot_general(
            same, glo.astype(BF16), nt, preferred_element_type=F32
        )
        pcol[r, :, pl.ds(0, 8)] = jnp.where(named_c > 0.5, rank_c, -4096.0)
        pcol[r, :, pl.ds(8, 8)] = gate_c

    crow = lax.broadcasted_iota(jnp.int32, (p.rows, tok_n), 0).astype(F32)
    dc = {}

    def dispatch(h):
        for j in list(range(1, ny)) + [0]:
            total = jnp.zeros((p.rows, p.d), F32)
            for i, r in enumerate(p.groups[h]):
                pick = jnp.where(prow[r, j : j + 1, :] + float(i * p.cap) == crow, 1.0, 0.0).astype(BF16)
                total = total + jnp.dot(pick, tokb[r, pl.ds(0, tok_n)], preferred_element_type=F32)
            total = total.astype(BF16)
            if j == 0:
                recvd[pl.ds(h * ny * p.rows, p.rows)] = total
            else:
                n = h * (ny - 1) + j - 1
                sendb[n] = total
                pos = p.yorder.index((ny - j) % ny)
                at = pl.ds((h * ny + pos) * p.rows, p.rows)
                dc[h, pos] = go(sendb.at[n], recvd.at[at], ds.at[n], dr.at[n], above[j])

    ec = {}

    def expert(h, first, count):
        base = (h * ny + first) * p.rows
        size = count * p.rows
        for pos in range(first, first + count):
            if pos > 0:
                dc[h, pos].arrive()

        def matrix(c, i):
            rows = pl.ds(i * p.d, p.d)
            return jnp.concatenate([wall[c, 0, rows], wall[c, 1, rows]], axis=1)

        def chunk(c, carry):
            xin = recvd[pl.ds(base, size)]
            g = jnp.dot(xin, matrix(c, 0), preferred_element_type=F32)
            u = jnp.dot(xin, matrix(c, 1), preferred_element_type=F32)
            hid = (g / (1.0 + jnp.exp(-g)) * u).astype(BF16)
            add = lax.dot_general(hid, matrix(c, 2), nt, preferred_element_type=F32)
            acc[pl.ds(0, size)] = acc[pl.ds(0, size)] + add
            return carry

        acc[pl.ds(0, size)] = jnp.zeros((size, p.d), F32)
        lax.fori_loop(0, nx, chunk, 0)
        res[pl.ds(base, size)] = acc[pl.ds(0, size)].astype(BF16)
        for pos in range(first, first + count):
            if pos > 0:
                o = p.yorder[pos]
                j = ny - o
                n = h * (ny - 1) + j - 1
                at = pl.ds((h * ny + pos) * p.rows, p.rows)
                ec[h, j] = go(res.at[at], rret.at[n], es.at[n], er.at[n], above[o])

    ccol = lax.broadcasted_iota(jnp.int32, (tok_n, p.rows), 1).astype(F32)

    def combine(r):
        h = 0 if r in p.groups[0] else 1
        i = p.groups[h].index(r)
        total = jnp.zeros((tok_n, p.d), F32)
        for j in range(ny):
            pick = jnp.where(pcol[r, :, j : j + 1] + float(i * p.cap) == ccol, 1.0, 0.0).astype(BF16)
            rows = res[pl.ds(h * ny * p.rows, p.rows)] if j == 0 else rret[h * (ny - 1) + j - 1]
            total = total + pcol[r, :, 8 + j : 9 + j] * jnp.dot(pick, rows, preferred_element_type=F32)
        part[r] = total

    rc = {}

    def reduce_step(dist):
        for way, half, d in p.rs:
            if d == dist:
                n = p.rs.index((way, half, dist))
                first, size = p.rscut[half]
                total = part[dist if way == 0 else nz - dist, pl.ds(first, size)]
                if (way, half, dist + 1) in rc:
                    rc[way, half, dist + 1].arrive()
                    total = total + rsin[p.rs.index((way, half, dist + 1)), pl.ds(0, size)].astype(F32)
                rsout[n, pl.ds(0, size)] = total.astype(BF16)
                rows = pl.ds(0, size)
                rc[way, half, dist] = go(rsout.at[n, rows], rsin.at[n, rows], rss.at[n], rsr.at[n], along[way])

    places(0)
    for s in range(2, p.half + 1):
        ag_step(s)
        places(s - 1)
        places(nz - s + 1)
    dispatch(0)
    x_second()
    spread_ready()
    for way in (0, 1):
        agc[way, way, p.half].arrive()
    places(p.half)
    convey_next()
    dispatch(1)
    convey_next()
    x_third()
    x_ready()
    for h in (0, 1):
        for first in range(0, ny, 2):
            expert(h, first, min(2, ny - first))
            convey_next()
    for j in range(1, ny):
        ec[0, j].arrive()
    for r in p.groups[0]:
        combine(r)
        convey_next()
    convey_next(len(todo))
    choose(range(ny))
    for j in range(1, ny):
        ec[1, j].arrive()
    deliver()
    for dist in range(p.half, 0, -1):
        for r in sorted({dist, nz - dist}):
            if r in p.groups[1]:
                combine(r)
        reduce_step(dist)
    for half in (0, 1):
        first, size = p.rscut[half]
        total = part[0, pl.ds(first, size)]
        for way in (0, 1):
            rc[way, half, 1].arrive()
            total = total + rsin[p.rs.index((way, half, 1)), pl.ds(0, size)].astype(F32)
        out[pl.ds(first, size)] = total.astype(BF16)
    for link in started:
        link.arrive()
    fc[-1].wait()
    for link in started:
        link.copy.wait_send()


def moe(p, *operands):
    ny, nz, nx = p.ny, p.nz, p.nx
    dma = pltpu.SemaphoreType.DMA
    vmem = pl.BlockSpec(memory_space=pltpu.VMEM)
    smem = pl.BlockSpec(memory_space=pltpu.SMEM)
    anywhere = pl.BlockSpec(memory_space=pl.ANY)
    wrows = 3 * p.d
    return pl.pallas_call(
        functools.partial(moe_kernel, p),
        out_shape=(
            jax.ShapeDtypeStruct((p.tok, p.d), BF16),
            jax.ShapeDtypeStruct((ny, p.piece, p.hs), BF16),
        ),
        in_specs=[anywhere, vmem, vmem, smem, smem, anywhere, anywhere, anywhere],
        out_specs=(vmem, anywhere),
        scratch_shapes=[
            pltpu.VMEM((nz, p.tok + META, p.d), BF16),
            pltpu.VMEM((2 * (ny - 1), p.rows, p.d), BF16),
            pltpu.VMEM((2 * ny * p.rows, p.d), BF16),
            pltpu.VMEM((nx, 2, wrows, p.hs), BF16),
            pltpu.VMEM((2 * ny * p.rows, p.d), BF16),
            pltpu.VMEM((2 * (ny - 1), p.rows, p.d), BF16),
            pltpu.VMEM((nz, p.tok, p.d), F32),
            pltpu.VMEM((len(p.rs), p.tok // 2, p.d), BF16),
            pltpu.VMEM((len(p.rs), p.tok // 2, p.d), BF16),
            pltpu.VMEM((2 * p.rows, p.d), F32),
            pltpu.VMEM((nz, 8, p.tok), F32),
            pltpu.VMEM((nz, p.tok, 128), F32),
            pltpu.VMEM((2, wrows, p.hs), F32),
            pltpu.VMEM((3 * wrows, p.hs), BF16),
            pltpu.VMEM((ny, p.piece, p.hs), BF16),
            pltpu.VMEM((4 * p.steps, p.chunk, p.hs), BF16),
            pltpu.VMEM((4 * p.steps, p.chunk, p.hs), BF16),
            pltpu.VMEM((ny, p.piece, p.hs), BF16),
            dma((7,)),
            dma((len(p.ag),)),
            dma((len(p.ag),)),
            dma((8,)),
            dma((8,)),
            dma((2 * (ny - 1),)),
            dma((2 * (ny - 1),)),
            dma((2 * (ny - 1),)),
            dma((2 * (ny - 1),)),
            dma((len(p.rs),)),
            dma((len(p.rs),)),
            dma((ny - 1,)),
            dma((ny - 1,)),
            dma((4 * p.steps,)),
            dma((4 * p.steps,)),
            dma((ny - 1,)),
            dma((ny - 1,)),
        ],
        compiler_params=pltpu.CompilerParams(
            collective_id=0, has_side_effects=True, vmem_limit_bytes=60 * 1024 * 1024
        ),
        name="moe",
    )(*operands)


def per_device(n_y, tokens, route_ids, gate_weight, old_owner, new_owner, weights, first_moment, second_moment):
    n = lax.axis_size("expert")
    tok, d = tokens.shape
    hs = weights.shape[3]
    p = Plan(lax.axis_size("dp"), n_y, n // n_y, tok, 3 * tok * route_ids.shape[1] // (2 * n), d, hs)
    layer_output, moved = moe(
        p,
        tokens,
        route_ids.T,
        gate_weight.T,
        old_owner,
        new_owner,
        weights.reshape(-1, hs),
        first_moment.reshape(-1, hs),
        second_moment.reshape(-1, hs),
    )
    moved = moved.reshape((3, *weights.shape))
    me = lax.axis_index("expert")
    stays = jnp.any((old_owner == me) & (new_owner == me))
    return (
        layer_output,
        jnp.where(stays, weights, moved[0]),
        jnp.where(stays, first_moment, moved[1].astype(F32)),
        jnp.where(stays, second_moment, moved[2].astype(F32)),
    )


def solution(mesh):
    experts = mesh.shape["expert"]
    n_y = 4 if experts == 32 else 2
    placed = (
        P(("dp", "expert"), None),
        P(("dp", "expert"), None),
        P(("dp", "expert"), None),
        P(),
        P(),
        P("expert", None, None, "dp"),
        P("expert", None, None, "dp"),
        P("expert", None, None, "dp"),
    )
    return jax.shard_map(
        functools.partial(per_device, n_y),
        mesh=mesh,
        in_specs=placed,
        out_specs=(
            P(("dp", "expert"), None),
            P("expert", None, None, "dp"),
            P("expert", None, None, "dp"),
            P("expert", None, None, "dp"),
        ),
        check_vma=False,
    )
```

time: 276 us -> 153 us (0.55)
  waiting for transfers between devices: 57.1 us -> 0 us
  Pallas kernels: 186 us -> 142 us
  starting transfers between devices: 15.8 us -> 0 us
    all_to_all x2 -> x0, waiting for transfers between devices: 57.1 us -> none  [the longest x1 57.1 us: moves(): lax.all_to_all(block, 'expert', split_axis=0, concat_axis=0, tiled=True)]
    pallas_call x2 -> x1, Pallas kernels: 186 us -> 142 us  [moe(): pl.pallas_call(functools.partial(moe_kernel, p), out_shape=(jax.ShapeDtyp...]
    all_to_all x2 -> x0, starting transfers between devices: 15.8 us -> none  [the longest x1 11.6 us: moves(): lax.all_to_all(block, 'expert', split_axis=0, concat_axis=0, tiled=True)]
  transfers between devices with their start and end apart: 2 -> 0, of which waited for: 1 -> 0; matrix products, arithmetic and copies ran while one was open for 1% -> 0% of each run, Pallas kernels for 62% -> 0%
where the time goes in v3:
time: 153 us; the launch traced here: 152 us
  Pallas kernels  142 us (93%)
  other arithmetic  8.25 us (5%)
    pallas_call x1, Pallas kernels, moe(): pl.pallas_call(functools.partial(moe_kernel, p), out_shape=(jax.ShapeDtyp...  142 us
    select_n x1, other arithmetic, per_device(): jnp.where(stays, second_moment, moved[2].astype(F32))  4.08 us

profile of v3, /device:TPU:2, one launch (start us, length us, event | category | flops | bytes accessed | tf_op | source)
XLA Modules:
  0.0 151.5 jit_solution(13623125925573828608)
XLA Ops:
  0.6 1.3 and_reduce_fusion
  1.9 0.0 copy-start.2
  1.9 0.0 copy-start.1
  2.0 141.9 %moe.1 = (bf16[192,1024]{1,0:T(8,128)(2,1)}, bf16[4,2304,128]{2,1,0:T(8,128)(2,1)}) custom-call(bf16[192,1024]{1,0:T(8,128)(2,1)} %tokens.1, s32[4,192]{1,0:T(4,128)} %bitcast.27, f32[4,192]{1,0:T(4,128)} %bitcast.28, s32[32]{0:T(128)} %old.1, s32[32]{0:T(128)} %new.1, bf16[3072,128]{1,0:T(8,128)(2,1)} %bitcast.24, f32[3072,128]{1,0:T(8,128)} %bitcast.22, ...), custom_call_target="tpu_custom_call" | custom-call | tf_op jit(solution)/shard_map/moe/pallas_call | solution.py:493
  143.8 0.0 copy-start
  143.8 0.0 copy-done.2
  143.9 2.9 %fusion = bf16[1,3,1024,128]{3,2,1,0:T(8,128)(2,1)} fusion(bf16[1,3,1024,128]{3,2,1,0:T(8,128)(2,1)S(1)} %copy-done.2, bf16[3,1,3,1024,128]{4,3,2,1,0:T(8,128)(2,1)} %bitcast.25, pred[]{:T(512)} %and_reduce_fusion), kind=kLoop, calls=%fused_computation.5 | loop fusion | flops 393216 | bytes 2359297 | tf_op jit(solution)/shard_map/jit(_where)/select_n | solution.py:566
  146.7 0.0 copy-done.1
  146.7 0.0 copy-done
  146.7 0.0 copy-start.3
  146.7 4.1 %convert_select_fusion = (f32[1,3,1024,128]{3,2,1,0:T(8,128)}, f32[1,3,1024,128]{3,2,1,0:T(8,128)}) fusion(f32[1,3,1024,128]{3,2,1,0:T(8,128)S(1)} %copy-done.1, bf16[3,1,3,1024,128]{4,3,2,1,0:T(8,128)(2,1)} %bitcast.26, pred[]{:T(512)} %and_reduce_fusion, f32[1,3,1024,128]{3,2,1,0:T(8,128)S(1)} %copy-done), kind=kLoop, calls=%fused_computation | loop fusion | flops 1572864 | bytes 7864321 | tf_op jit(solution)/shard_map/jit(_where)/select_n | solution.py:568
  150.8 0.0 copy-done.3
  150.8 0.7 copy.16
Async XLA Ops:
  1.9 141.9 %copy-start.2 = (bf16[1,3,1024,128]{3,2,1,0:T(8,128)(2,1)S(1)}, bf16[1,3,1024,128]{3,2,1,0:T(8,128)(2,1)}, u32[]{:S(2)}) copy-start(bf16[1,3,1024,128]{3,2,1,0:T(8,128)(2,1)} %param.13) | copy-start | bytes 2359300
  1.9 144.8 %copy-start.1 = (f32[1,3,1024,128]{3,2,1,0:T(8,128)S(1)}, f32[1,3,1024,128]{3,2,1,0:T(8,128)}, u32[]{:S(2)}) copy-start(f32[1,3,1024,128]{3,2,1,0:T(8,128)} %param.15) | copy-start | bytes 4718596
  143.8 2.9 %copy-start = (f32[1,3,1024,128]{3,2,1,0:T(8,128)S(1)}, f32[1,3,1024,128]{3,2,1,0:T(8,128)}, u32[]{:S(2)}) copy-start(f32[1,3,1024,128]{3,2,1,0:T(8,128)} %param.14) | copy-start | bytes 4718596
  146.7 4.1 %copy-start.3 = (bf16[192,1024]{1,0:T(8,128)(2,1)S(1)}, bf16[192,1024]{1,0:T(8,128)(2,1)}, u32[]{:S(2)}) copy-start(bf16[192,1024]{1,0:T(8,128)(2,1)} %get-tuple-element.14) | copy-start | bytes 1179652

commit v4 on v3

--- a/solution.py
+++ b/solution.py
@@ -11,6 +11,8 @@
 F32 = jnp.float32
 BF16 = jnp.bfloat16
 META = 16
+FAR_FIRST = False
+EARLY = False
 
 
 class Plan:
@@ -30,20 +32,20 @@
         self.piece = 9 * d // n_y
         self.chunk = self.piece // self.chunks
         cut = tok // 2
-        self.agcut = ((0, cut), (cut, tok + META - cut))
+        self.agcut = ((0, cut), (cut, tok - cut))
         self.rscut = ((0, cut), (cut, tok - cut))
         self.ag = [
             (way, part, s)
             for s in range(1, self.half + 1)
+            for part in (0, 1, 2)
             for way in (0, 1)
-            for part in (0, 1)
-            if s < self.half or way == part
+            if s < self.half or way == part % 2
         ]
         self.rs = [
             (way, part, dist)
             for dist in range(self.half, 0, -1)
+            for part in (0, 1)
             for way in (0, 1)
-            for part in (0, 1)
             if dist < self.half or way == part
         ]
 
@@ -75,6 +77,7 @@
     out,
     moved,
     tokb,
+    metab,
     sendb,
     recvd,
     wall,
@@ -135,7 +138,7 @@
         copy.start()
         return copy
 
-    own_tokens = local(0, tokens, tokb.at[0, pl.ds(0, tok_n)])
+    own_tokens = local(0, tokens, tokb.at[0])
     own_weights = local(1, wts, wall.at[0, 0])
     wrows = 3 * p.d
     block_weights = local(2, wts, block.at[pl.ds(0, wrows)])
@@ -153,10 +156,13 @@
     def ag_send(way, half, s):
         src = (nz - (s - 1)) % nz if way == 0 else s - 1
         dst = nz - s if way == 0 else s
-        rows = pl.ds(*p.agcut[half])
         n = p.ag.index((way, half, s))
-        source = tokens.at[rows] if (s, half) == (1, 0) else tokb.at[src, rows]
-        agc[way, half, s] = go(source, tokb.at[dst, rows], ags.at[n], agr.at[n], along[way])
+        if half == 2:
+            agc[way, half, s] = go(metab.at[src], metab.at[dst], ags.at[n], agr.at[n], along[way])
+        else:
+            rows = pl.ds(*p.agcut[half])
+            source = tokens.at[rows] if s == 1 else tokb.at[src, rows]
+            agc[way, half, s] = go(source, tokb.at[dst, rows], ags.at[n], agr.at[n], along[way])
 
     def ag_step(s):
         for way, half, step in p.ag:
@@ -167,8 +173,9 @@
             if step == s - 1:
                 agc[way, half, step].arrive()
 
-    for way in (0, 1):
-        ag_send(way, 0, 1)
+    for half in (0, 1):
+        for way in (0, 1):
+            ag_send(way, half, 1)
 
     xc = [go(wts, wall.at[0, 1], xs.at[0], xr.at[0], twin)]
     if nx > 1:
@@ -205,12 +212,9 @@
     wide = -(-tok_n // 128) * 128
     if wide > tok_n:
         meta = jnp.concatenate([meta, jnp.zeros((META, wide - tok_n), F32)], axis=1)
-    tokb[0, pl.ds(tok_n, META), pl.ds(0, wide)] = meta.astype(BF16)
-    if wide < p.d:
-        tokb[0, pl.ds(tok_n, META), pl.ds(wide, p.d - wide)] = jnp.zeros((META, p.d - wide), BF16)
-    own_tokens.wait()
+    metab[0] = meta.astype(BF16)
     for way in (0, 1):
-        ag_send(way, 1, 1)
+        ag_send(way, 2, 1)
 
     block_weights.wait()
     stage_first.wait()
@@ -335,7 +339,7 @@
     nt = (((1,), (1,)), ((), ()))
 
     def places(r):
-        m = tokb[r, pl.ds(tok_n, META), pl.ds(0, tok_n)].astype(F32)
+        m = metab[r, :, pl.ds(0, tok_n)].astype(F32)
         named = jnp.zeros((8, tok_n), F32)
         ghi = jnp.zeros((8, tok_n), F32)
         glo = jnp.zeros((8, tok_n), F32)
@@ -359,11 +363,11 @@
     dc = {}
 
     def dispatch(h):
-        for j in list(range(1, ny)) + [0]:
+        for j in [(ny - o) % ny for o in p.yorder[1:] + p.yorder[:1]]:
             total = jnp.zeros((p.rows, p.d), F32)
             for i, r in enumerate(p.groups[h]):
                 pick = jnp.where(prow[r, j : j + 1, :] + float(i * p.cap) == crow, 1.0, 0.0).astype(BF16)
-                total = total + jnp.dot(pick, tokb[r, pl.ds(0, tok_n)], preferred_element_type=F32)
+                total = total + jnp.dot(pick, tokb[r], preferred_element_type=F32)
             total = total.astype(BF16)
             if j == 0:
                 recvd[pl.ds(h * ny * p.rows, p.rows)] = total
@@ -397,8 +401,12 @@
             return carry
 
         acc[pl.ds(0, size)] = jnp.zeros((size, p.d), F32)
-        lax.fori_loop(0, nx, chunk, 0)
+        for part in range(0, nx, 2):
+            lax.fori_loop(part, min(part + 2, nx), chunk, 0)
+            convey_next()
         res[pl.ds(base, size)] = acc[pl.ds(0, size)].astype(BF16)
+
+    def answer(h, first, count):
         for pos in range(first, first + count):
             if pos > 0:
                 o = p.yorder[pos]
@@ -434,41 +442,61 @@
                 rows = pl.ds(0, size)
                 rc[way, half, dist] = go(rsout.at[n, rows], rsin.at[n, rows], rss.at[n], rsr.at[n], along[way])
 
+    halves = [(first, min(2, ny - first)) for first in range(0, ny, 2)]
     places(0)
     for s in range(2, p.half + 1):
         ag_step(s)
         places(s - 1)
         places(nz - s + 1)
-    dispatch(0)
-    x_second()
+        if s == max(2, p.half - 1):
+            own_tokens.wait()
+            dispatch(0)
+            x_second()
     spread_ready()
-    for way in (0, 1):
-        agc[way, way, p.half].arrive()
+    convey_next()
+    for half in (0, 1, 2):
+        agc[half % 2, half, p.half].arrive()
     places(p.half)
-    convey_next()
     dispatch(1)
     convey_next()
     x_third()
     x_ready()
     for h in (0, 1):
-        for first in range(0, ny, 2):
-            expert(h, first, min(2, ny - first))
-            convey_next()
-    for j in range(1, ny):
-        ec[0, j].arrive()
-    for r in p.groups[0]:
-        combine(r)
-        convey_next()
+        for span in halves:
+            expert(h, *span)
+            if h == 1 or not FAR_FIRST:
+                answer(h, *span)
+    if FAR_FIRST:
+        for span in halves:
+            answer(0, *span)
     convey_next(len(todo))
     choose(range(ny))
+    if EARLY:
+        deliver()
+    if not FAR_FIRST:
+        for j in range(1, ny):
+            ec[0, j].arrive()
+        for r in p.groups[0]:
+            combine(r)
     for j in range(1, ny):
         ec[1, j].arrive()
-    deliver()
+    if not EARLY and not FAR_FIRST:
+        deliver()
     for dist in range(p.half, 0, -1):
-        for r in sorted({dist, nz - dist}):
-            if r in p.groups[1]:
+        pair = sorted({dist, nz - dist})
+        if FAR_FIRST and pair[0] in p.groups[0] and not fc:
+            for j in range(1, ny):
+                ec[0, j].arrive()
+            deliver()
+        elif FAR_FIRST and pair[0] in p.groups[0]:
+            for j in range(1, ny):
+                ec[0, j].arrive()
+        for r in pair:
+            if FAR_FIRST or r in p.groups[1]:
                 combine(r)
         reduce_step(dist)
+    if FAR_FIRST:
+        combine(0)
     for half in (0, 1):
         first, size = p.rscut[half]
         total = part[0, pl.ds(first, size)]
@@ -499,7 +527,8 @@
         in_specs=[anywhere, vmem, vmem, smem, smem, anywhere, anywhere, anywhere],
         out_specs=(vmem, anywhere),
         scratch_shapes=[
-            pltpu.VMEM((nz, p.tok + META, p.d), BF16),
+            pltpu.VMEM((nz, p.tok, p.d), BF16),
+            pltpu.VMEM((nz, META, -(-p.tok // 128) * 128), BF16),
             pltpu.VMEM((2 * (ny - 1), p.rows, p.d), BF16),
             pltpu.VMEM((2 * ny * p.rows, p.d), BF16),
             pltpu.VMEM((nx, 2, wrows, p.hs), BF16),
@@ -542,31 +571,94 @@
     )(*operands)
 
 
+def finish_kernel(n, d, old, new, layer, wts, first_m, second_m, moved, out, w_out, f_out, s_out, lbuf, wbuf, half, full, sems):
+    me = lax.axis_index("expert")
+    rows = 3 * d
+    cut = rows // 4
+
+    def look(e, found):
+        return jnp.where((old[e] == me) & (new[e] == me), 1, found)
+
+    layer_in = pltpu.make_async_copy(layer, lbuf, sems.at[0])
+    layer_in.start()
+    stays = lax.fori_loop(0, n, look, 0) == 1
+
+    def run(sources):
+        parts = []
+        for a, (src, base, mid, end, dst) in enumerate(sources):
+            for i in range(4):
+                at = pl.ds(i * cut, cut)
+                load = pltpu.make_async_copy(src.at[pl.ds(base + i * cut, cut)], mid.at[at], sems.at[2 + a * 4 + i])
+                load.start()
+                parts.append((load, mid, end, dst, at, sems.at[14 + a * 4 + i]))
+        stores = []
+        for load, mid, end, dst, at, sem in parts:
+            load.wait()
+            if end is not mid:
+                end[at] = mid[at].astype(F32)
+            store = pltpu.make_async_copy(end.at[at], dst.at[at], sem)
+            store.start()
+            stores.append(store)
+        for store in stores:
+            store.wait()
+
+    @pl.when(stays)
+    def _():
+        one, two = full.at[0], full.at[1]
+        run(((wts, 0, wbuf, wbuf, w_out), (first_m, 0, one, one, f_out), (second_m, 0, two, two, s_out)))
+
+    @pl.when(jnp.logical_not(stays))
+    def _():
+        run(
+            (
+                (moved, 0, wbuf, wbuf, w_out),
+                (moved, rows, half.at[0], full.at[0], f_out),
+                (moved, 2 * rows, half.at[1], full.at[1], s_out),
+            )
+        )
+
+    layer_in.wait()
+    layer_out = pltpu.make_async_copy(lbuf, out, sems.at[1])
+    layer_out.start()
+    layer_out.wait()
+
+
+def finish(n, d, *operands):
+    layer, wts = operands[2], operands[3]
+    smem = pl.BlockSpec(memory_space=pltpu.SMEM)
+    anywhere = pl.BlockSpec(memory_space=pl.ANY)
+    rows, lanes = wts.shape
+    return pl.pallas_call(
+        functools.partial(finish_kernel, n, d),
+        out_shape=(
+            jax.ShapeDtypeStruct(layer.shape, layer.dtype),
+            jax.ShapeDtypeStruct(wts.shape, BF16),
+            jax.ShapeDtypeStruct(wts.shape, F32),
+            jax.ShapeDtypeStruct(wts.shape, F32),
+        ),
+        in_specs=[smem, smem] + [anywhere] * 5,
+        out_specs=[anywhere] * 4,
+        scratch_shapes=[
+            pltpu.VMEM(layer.shape, BF16),
+            pltpu.VMEM((rows, lanes), BF16),
+            pltpu.VMEM((2, rows, lanes), BF16),
+            pltpu.VMEM((2, rows, lanes), F32),
+            pltpu.SemaphoreType.DMA((26,)),
+        ],
+        compiler_params=pltpu.CompilerParams(vmem_limit_bytes=60 * 1024 * 1024),
+        name="finish",
+    )(*operands)
+
+
 def per_device(n_y, tokens, route_ids, gate_weight, old_owner, new_owner, weights, first_moment, second_moment):
     n = lax.axis_size("expert")
     tok, d = tokens.shape
     hs = weights.shape[3]
     p = Plan(lax.axis_size("dp"), n_y, n // n_y, tok, 3 * tok * route_ids.shape[1] // (2 * n), d, hs)
-    layer_output, moved = moe(
-        p,
-        tokens,
-        route_ids.T,
-        gate_weight.T,
-        old_owner,
-        new_owner,
-        weights.reshape(-1, hs),
-        first_moment.reshape(-1, hs),
-        second_moment.reshape(-1, hs),
-    )
-    moved = moved.reshape((3, *weights.shape))
-    me = lax.axis_index("expert")
-    stays = jnp.any((old_owner == me) & (new_owner == me))
-    return (
-        layer_output,
-        jnp.where(stays, weights, moved[0]),
-        jnp.where(stays, first_moment, moved[1].astype(F32)),
-        jnp.where(stays, second_moment, moved[2].astype(F32)),
-    )
+    blocks = [a.reshape(-1, hs) for a in (weights, first_moment, second_moment)]
+    layer, moved = moe(p, tokens, route_ids.T, gate_weight.T, old_owner, new_owner, *blocks)
+    done = finish(n, d, old_owner, new_owner, layer, *blocks, moved.reshape(-1, hs))
+    return (done[0], *(a.reshape(weights.shape) for a in done[1:]))
 
 
 def solution(mesh):

time: 153 us -> 137 us (0.90)
  other arithmetic: 8.25 us -> 0 us
  Pallas kernels: 142 us -> 136 us
    pallas_call x1, Pallas kernels: 142 us -> 131 us  [moe(): pl.pallas_call(functools.partial(moe_kernel, p), out_shape=(jax.ShapeDtyp...]
    select_n x2 -> x0, other arithmetic: 6.94 us -> none  [the longest x1 4.08 us: per_device(): jnp.where(stays, second_moment, moved[2].astype(F32))]
    pallas_call x0 -> x1, Pallas kernels: none -> 5.4 us  [finish(): pl.pallas_call(functools.partial(finish_kernel, n, d), out_shape=(jax.Sha...]
where the time goes in v4:
time: 137 us
  Pallas kernels  136 us (99%)
    pallas_call x1, Pallas kernels, moe(): pl.pallas_call(functools.partial(moe_kernel, p), out_shape=(jax.ShapeDtyp...  131 us
    pallas_call x1, Pallas kernels, finish(): pl.pallas_call(functools.partial(finish_kernel, n, d), out_shape=(jax.Sha...  5.4 us

profile of v4, /device:TPU:2, one launch (start us, length us, event | category | flops | bytes accessed | tf_op | source)
XLA Modules:
  0.0 137.1 jit_solution(14687157530813717633)
XLA Ops:
  0.6 130.9 %moe.1 = (bf16[192,1024]{1,0:T(8,128)(2,1)}, bf16[4,2304,128]{2,1,0:T(8,128)(2,1)}) custom-call(bf16[192,1024]{1,0:T(8,128)(2,1)} %tokens.1, s32[4,192]{1,0:T(4,128)} %bitcast.16, f32[4,192]{1,0:T(4,128)} %bitcast.17, s32[32]{0:T(128)} %old.3, s32[32]{0:T(128)} %new.3, bf16[3072,128]{1,0:T(8,128)(2,1)} %bitcast.13, f32[3072,128]{1,0:T(8,128)} %bitcast.9, ...), custom_call_target="tpu_custom_call" | custom-call | tf_op jit(solution)/shard_map/moe/pallas_call | solution.py:521
  131.5 5.4 %finish.1 = (bf16[192,1024]{1,0:T(8,128)(2,1)}, bf16[3072,128]{1,0:T(8,128)(2,1)}, f32[3072,128]{1,0:T(8,128)}, f32[3072,128]{1,0:T(8,128)}) custom-call(s32[32]{0:T(128)} %old.3, s32[32]{0:T(128)} %new.3, bf16[192,1024]{1,0:T(8,128)(2,1)} %get-tuple-element.10.layer, bf16[3072,128]{1,0:T(8,128)(2,1)} %bitcast.14, f32[3072,128]{1,0:T(8,128)} %bitcast.10, ...), custom_call_target="tpu_custom_call" | custom-call | tf_op jit(solution)/shard_map/finish/pallas_call | solution.py:631

commit v5 on v4

--- a/solution.py
+++ b/solution.py
@@ -11,7 +11,7 @@
 F32 = jnp.float32
 BF16 = jnp.bfloat16
 META = 16
-FAR_FIRST = False
+FAR_FIRST = True
 EARLY = False
 
 
@@ -27,7 +27,7 @@
         self.groups = (order[: self.half], order[self.half :])
         self.rows = self.half * cap
         self.yorder = [0, 1, 3, 2] if n_y == 4 else list(range(n_y))
-        self.chunks = 8
+        self.chunks = 6
         self.steps = self.chunks + self.half - 1
         self.piece = 9 * d // n_y
         self.chunk = self.piece // self.chunks
@@ -91,7 +91,8 @@
     pcol,
     stage,
     block,
-    spread,
+    spread0,
+    spread1,
     cin,
     cout,
     fin,
@@ -149,6 +150,30 @@
     peers = [right, left, twin] + above[1:] + ([xright, xleft] if nx > 1 else [])
     for peer in peers:
         pl.semaphore_signal(barrier, inc=1, device_id=peer, device_id_type=MESH)
+    slots = jnp.zeros((4, tok_n), jnp.int32)
+    for e in range(ny * nz):
+        slots = jnp.where(route[...] == e, old[e], slots)
+    g = gate[...]
+    high = g.astype(BF16).astype(F32)
+    meta = jnp.concatenate([slots.astype(F32), high, g - high, jnp.full((4, tok_n), -1.0, F32)], axis=0)
+    wide = -(-tok_n // 128) * 128
+    if wide > tok_n:
+        meta = jnp.concatenate([meta, jnp.zeros((META, wide - tok_n), F32)], axis=1)
+    metab[0] = meta.astype(BF16)
+    block_weights.wait()
+    stage_first.wait()
+    stage_second.wait()
+    step_rows = 256
+
+    def narrow(i, carry):
+        for a in (0, 1):
+            rows = pl.ds(pl.multiple_of(i * step_rows, step_rows), step_rows)
+            to = pl.ds(pl.multiple_of((1 + a) * wrows + i * step_rows, step_rows), step_rows)
+            block[to] = stage[a, rows].astype(BF16)
+        return carry
+
+    lax.fori_loop(0, wrows // step_rows, narrow, 0)
+
     pl.semaphore_wait(barrier, len(peers))
 
     agc = {}
@@ -173,9 +198,22 @@
             if step == s - 1:
                 agc[way, half, step].arrive()
 
-    for half in (0, 1):
+    for half in (0, 1, 2):
         for way in (0, 1):
             ag_send(way, half, 1)
+
+    hp = p.piece // 2
+
+    def piece(i, part):
+        return block.at[pl.ds(pl.multiple_of(i * p.piece + part * hp, hp), hp)]
+
+    spread = (spread0, spread1)
+    keep_piece = [local(5 + 2 * part, piece(y, part), spread[part].at[y]) for part in (0, 1)]
+    sc = ([], [])
+    for cut in (0, 1):
+        for j in range(1, ny):
+            n = cut * (ny - 1) + j - 1
+            sc[cut].append(go(piece((y + j) % ny, cut), spread[cut].at[y], ss.at[n], sr.at[n], above[j]))
 
     xc = [go(wts, wall.at[0, 1], xs.at[0], xr.at[0], twin)]
     if nx > 1:
@@ -203,43 +241,16 @@
         for link in xc:
             link.arrive()
 
-    slots = jnp.zeros((4, tok_n), jnp.int32)
-    for e in range(ny * nz):
-        slots = jnp.where(route[...] == e, old[e], slots)
-    g = gate[...]
-    high = g.astype(BF16).astype(F32)
-    meta = jnp.concatenate([slots.astype(F32), high, g - high, jnp.full((4, tok_n), -1.0, F32)], axis=0)
-    wide = -(-tok_n // 128) * 128
-    if wide > tok_n:
-        meta = jnp.concatenate([meta, jnp.zeros((META, wide - tok_n), F32)], axis=1)
-    metab[0] = meta.astype(BF16)
-    for way in (0, 1):
-        ag_send(way, 2, 1)
-
-    block_weights.wait()
-    stage_first.wait()
-    stage_second.wait()
-    step_rows = 256
-
-    def narrow(i, carry):
-        for a in (0, 1):
-            rows = pl.ds(pl.multiple_of(i * step_rows, step_rows), step_rows)
-            to = pl.ds(pl.multiple_of((1 + a) * wrows + i * step_rows, step_rows), step_rows)
-            block[to] = stage[a, rows].astype(BF16)
-        return carry
-
-    lax.fori_loop(0, wrows // step_rows, narrow, 0)
-
-    def piece(i):
-        return block.at[pl.ds(pl.multiple_of(i * p.piece, p.piece), p.piece)]
-
-    keep_piece = local(5, piece(y), spread.at[y])
-    sc = [go(piece((y + j) % ny), spread.at[y], ss.at[j - 1], sr.at[j - 1], above[j]) for j in range(1, ny)]
-
-    def spread_ready():
-        keep_piece.wait()
-        for link in sc:
+
+    def spread_ready(part):
+        if not sc[part][0].here:
+            keep_piece[part].wait()
+        for link in sc[part]:
             link.arrive()
+
+    def spread_rows(t):
+        part = t * p.chunk // hp
+        return spread[part], pl.ds(t * p.chunk - part * hp, p.chunk)
 
     def scan(e, carry):
         seen, named = carry
@@ -283,14 +294,17 @@
             for way in (0, 1):
                 n = (way * 2 + lane) * p.steps + t
                 mine, ysrc, second = lanes[way, lane]
+                if t < p.chunks:
+                    spread_ready(t * p.chunk // hp)
+                    pieces, rows = spread_rows(t)
                 if t > 0:
                     for inlane in (0, 1):
                         cc[way, inlane, t - 1].arrive()
                     value = jnp.where(second, cin[(way * 2 + 1) * p.steps + t - 1], cin[way * 2 * p.steps + t - 1])
                     if t < p.chunks:
-                        value = jnp.where(mine, spread[ysrc, pl.ds(t * p.chunk, p.chunk)], value)
+                        value = jnp.where(mine, pieces[ysrc, rows], value)
                 else:
-                    value = spread[ysrc, pl.ds(0, p.chunk)]
+                    value = pieces[ysrc, rows]
                 cout[n] = value
                 cc[way, lane, t] = go(cout.at[n], cin.at[n], cs.at[n], cr.at[n], along[way])
 
@@ -313,13 +327,17 @@
                 ysrc = jnp.where(here, other[2], ysrc)
                 at = jnp.where(here, other[3], at)
 
-            def one(k, carry):
-                rows = pl.ds(pl.multiple_of(k * p.chunk, p.chunk), p.chunk)
-                value = jnp.where(by_cw, cin[at + k], cin[2 * p.steps + at + k])
-                fin[j, rows] = jnp.where(stay, spread[ysrc, rows], value)
-                return carry
-
-            lax.fori_loop(0, p.chunks, one, 0)
+            for part in (0, 1):
+
+                def one(k, carry):
+                    rows = pl.ds(pl.multiple_of(k * p.chunk, p.chunk), p.chunk)
+                    t = part * (p.chunks // 2) + k
+                    value = jnp.where(by_cw, cin[at + t], cin[2 * p.steps + at + t])
+                    value = jnp.where(stay, spread[part][ysrc, rows], value)
+                    fin[j, pl.ds(pl.multiple_of(t * p.chunk, p.chunk), p.chunk)] = value
+                    return carry
+
+                lax.fori_loop(0, p.chunks // 2, one, 0)
 
     fc = []
 
@@ -403,7 +421,8 @@
         acc[pl.ds(0, size)] = jnp.zeros((size, p.d), F32)
         for part in range(0, nx, 2):
             lax.fori_loop(part, min(part + 2, nx), chunk, 0)
-            convey_next()
+            if part == 0:
+                convey_next()
         res[pl.ds(base, size)] = acc[pl.ds(0, size)].astype(BF16)
 
     def answer(h, first, count):
@@ -452,7 +471,7 @@
             own_tokens.wait()
             dispatch(0)
             x_second()
-    spread_ready()
+            convey_next()
     convey_next()
     for half in (0, 1, 2):
         agc[half % 2, half, p.half].arrive()
@@ -542,11 +561,12 @@
             pltpu.VMEM((nz, p.tok, 128), F32),
             pltpu.VMEM((2, wrows, p.hs), F32),
             pltpu.VMEM((3 * wrows, p.hs), BF16),
-            pltpu.VMEM((ny, p.piece, p.hs), BF16),
+            pltpu.VMEM((ny, p.piece // 2, p.hs), BF16),
+            pltpu.VMEM((ny, p.piece // 2, p.hs), BF16),
             pltpu.VMEM((4 * p.steps, p.chunk, p.hs), BF16),
             pltpu.VMEM((4 * p.steps, p.chunk, p.hs), BF16),
             pltpu.VMEM((ny, p.piece, p.hs), BF16),
-            dma((7,)),
+            dma((8,)),
             dma((len(p.ag),)),
             dma((len(p.ag),)),
             dma((8,)),
@@ -557,8 +577,8 @@
             dma((2 * (ny - 1),)),
             dma((len(p.rs),)),
             dma((len(p.rs),)),
-            dma((ny - 1,)),
-            dma((ny - 1,)),
+            dma((2 * (ny - 1),)),
+            dma((2 * (ny - 1),)),
             dma((4 * p.steps,)),
             dma((4 * p.steps,)),
             dma((ny - 1,)),

time: 137 us -> 132 us (0.964)
  Pallas kernels: 136 us -> 131 us
    pallas_call x1, Pallas kernels: 131 us -> 125 us  [moe(): pl.pallas_call(functools.partial(moe_kernel, p), out_shape=(jax.ShapeDtyp...]
where the time goes in v5:
time: 132 us
  Pallas kernels  131 us (99%)
    pallas_call x1, Pallas kernels, moe(): pl.pallas_call(functools.partial(moe_kernel, p), out_shape=(jax.ShapeDtyp...  125 us
    pallas_call x1, Pallas kernels, finish(): pl.pallas_call(functools.partial(finish_kernel, n, d), out_shape=(jax.Sha...  5.4 us

profile of v5, /device:TPU:2, one launch (start us, length us, event | category | flops | bytes accessed | tf_op | source)
XLA Modules:
  0.0 131.6 jit_solution(1147232835678896826)
XLA Ops:
  0.6 125.4 %moe.1 = (bf16[192,1024]{1,0:T(8,128)(2,1)}, bf16[4,2304,128]{2,1,0:T(8,128)(2,1)}) custom-call(bf16[192,1024]{1,0:T(8,128)(2,1)} %tokens.1, s32[4,192]{1,0:T(4,128)} %bitcast.16, f32[4,192]{1,0:T(4,128)} %bitcast.17, s32[32]{0:T(128)} %old.3, s32[32]{0:T(128)} %new.3, bf16[3072,128]{1,0:T(8,128)(2,1)} %bitcast.13, f32[3072,128]{1,0:T(8,128)} %bitcast.9, ...), custom_call_target="tpu_custom_call" | custom-call | tf_op jit(solution)/shard_map/moe/pallas_call | solution.py:540
  126.0 5.4 %finish.1 = (bf16[192,1024]{1,0:T(8,128)(2,1)}, bf16[3072,128]{1,0:T(8,128)(2,1)}, f32[3072,128]{1,0:T(8,128)}, f32[3072,128]{1,0:T(8,128)}) custom-call(s32[32]{0:T(128)} %old.3, s32[32]{0:T(128)} %new.3, bf16[192,1024]{1,0:T(8,128)(2,1)} %get-tuple-element.10.layer, bf16[3072,128]{1,0:T(8,128)(2,1)} %bitcast.14, f32[3072,128]{1,0:T(8,128)} %bitcast.10, ...), custom_call_target="tpu_custom_call" | custom-call | tf_op jit(solution)/shard_map/finish/pallas_call | solution.py:651

commit v6 on v5

--- a/solution.py
+++ b/solution.py
@@ -27,7 +27,7 @@
         self.groups = (order[: self.half], order[self.half :])
         self.rows = self.half * cap
         self.yorder = [0, 1, 3, 2] if n_y == 4 else list(range(n_y))
-        self.chunks = 6
+        self.chunks = 4
         self.steps = self.chunks + self.half - 1
         self.piece = 9 * d // n_y
         self.chunk = self.piece // self.chunks

time: 132 us -> 143 us (1.083)
  Pallas kernels: 131 us -> 142 us
    pallas_call x1, Pallas kernels: 125 us -> 136 us  [moe(): pl.pallas_call(functools.partial(moe_kernel, p), out_shape=(jax.ShapeDtyp...]
where the time goes in v6:
time: 143 us
  Pallas kernels  142 us (99%)
    pallas_call x1, Pallas kernels, moe(): pl.pallas_call(functools.partial(moe_kernel, p), out_shape=(jax.ShapeDtyp...  136 us
    pallas_call x1, Pallas kernels, finish(): pl.pallas_call(functools.partial(finish_kernel, n, d), out_shape=(jax.Sha...  5.4 us

profile of v6, /device:TPU:2, one launch (start us, length us, event | category | flops | bytes accessed | tf_op | source)
XLA Modules:
  0.0 142.5 jit_solution(18053428476565063393)
XLA Ops:
  0.6 136.3 %moe.1 = (bf16[192,1024]{1,0:T(8,128)(2,1)}, bf16[4,2304,128]{2,1,0:T(8,128)(2,1)}) custom-call(bf16[192,1024]{1,0:T(8,128)(2,1)} %tokens.1, s32[4,192]{1,0:T(4,128)} %bitcast.16, f32[4,192]{1,0:T(4,128)} %bitcast.17, s32[32]{0:T(128)} %old.3, s32[32]{0:T(128)} %new.3, bf16[3072,128]{1,0:T(8,128)(2,1)} %bitcast.13, f32[3072,128]{1,0:T(8,128)} %bitcast.9, ...), custom_call_target="tpu_custom_call" | custom-call | tf_op jit(solution)/shard_map/moe/pallas_call | solution.py:540
  136.9 5.4 %finish.1 = (bf16[192,1024]{1,0:T(8,128)(2,1)}, bf16[3072,128]{1,0:T(8,128)(2,1)}, f32[3072,128]{1,0:T(8,128)}, f32[3072,128]{1,0:T(8,128)}) custom-call(s32[32]{0:T(128)} %old.3, s32[32]{0:T(128)} %new.3, bf16[192,1024]{1,0:T(8,128)(2,1)} %get-tuple-element.10.layer, bf16[3072,128]{1,0:T(8,128)(2,1)} %bitcast.14, f32[3072,128]{1,0:T(8,128)} %bitcast.10, ...), custom_call_target="tpu_custom_call" | custom-call | tf_op jit(solution)/shard_map/finish/pallas_call | solution.py:651
